TPU v7x, 512 devices: a whole 4x4x16 slice. The times are simulated.
512 devices in a mesh: rep: 64 (over z, x_lo, core), tp: 8 (over y, x_hi).
Axes of the slice: x: 4 (x_hi: 2, x_lo: 2; x = x_hi * 2 + x_lo), y: 4, z: 16, core: 2. Of those that a mesh axis runs over, the one named last changes fastest.
Arguments:
- owner: int32 [8], replicated, may hold values from 0 to 63
- queries: bfloat16 [16384, 8192], P('rep', 'tp'), may hold values from -128 to 128
- rotated_suffix_keys: bfloat16 [16384, 1024], P('rep', 'tp'), may hold values from -16 to 16
- suffix_values: bfloat16 [16384, 1024], P('rep', 'tp'), may hold values from -6 to 6
- prefix_keys: bfloat16 [262144, 1024], P('rep', 'tp'), may hold values from -6 to 6
- prefix_values: bfloat16 [262144, 1024], P('rep', 'tp'), may hold values from -6 to 6
Outputs:
- context: bfloat16 [16384, 8192], P(('rep', 'tp'))
Inputs may be any that keep to these rules, and one draw needn't show every extreme that they name: `owner`: entry k is the replica whose rows of prefix_keys and prefix_values hold key and value head k of the prompt's cache.
All inputs are finite; a program needn't handle non-finite values.
Results may differ from a plain program's by a relative error of at most 0.0046.
Values may be sent and summed in bfloat16 or wider, within the bound.
No kernel may reach another device: no remote copies, remote signals or barrier semaphores. Data moves between devices by JAX's collectives and lax.ppermute only.
A program may use at most 64 MiB of HBM per device.

v0:
```python
import jax
import jax.numpy as jnp
from jax import lax
from jax.sharding import PartitionSpec as P

Q_HEADS = 64
KEY_VALUE_HEADS = 8
HEAD_WIDTH = 128
BLOCK = 512


def from_root(block, axis, owner):
    block = jnp.where(lax.axis_index(axis) == owner, block, jnp.zeros_like(block))
    return lax.psum(block, axis)


def block_partials(query_matrix, key_rows, value_rows, allowed, rescale_factor):
    count = key_rows.shape[0]
    heads_here = key_rows.shape[1] // HEAD_WIDTH
    key_split = key_rows.reshape(count, heads_here, HEAD_WIDTH)
    value_split = value_rows.reshape(count, heads_here, HEAD_WIDTH)
    scores = (
        jnp.einsum("ikgd,nkd->kgin", query_matrix, key_split, preferred_element_type=jnp.float32)
        * rescale_factor
    )
    if allowed is not None:
        scores = jnp.where(allowed, scores, jnp.float32(-1e30))
    largest = jnp.max(scores, axis=-1)
    weights = jnp.exp(scores - largest[..., None]).astype(jnp.bfloat16)
    total = jnp.sum(weights.astype(jnp.float32), axis=-1)
    partial_out = jnp.einsum(
        "kgin,nkd->kgid", weights, value_split, preferred_element_type=jnp.float32
    )
    return (largest, total, partial_out)


def combine_partials(running_state, largest, total, partial_out):
    running_max, running_total, running_out = running_state
    newest = jnp.maximum(running_max, largest)
    old_factor = jnp.exp(running_max - newest)
    new_factor = jnp.exp(largest - newest)
    return (
        newest,
        running_total * old_factor + total * new_factor,
        running_out * old_factor[..., None] + partial_out * new_factor[..., None],
    )


def local(owner, queries, rotated_suffix_keys, suffix_values, prefix_keys, prefix_values):
    suffix_rows = queries.shape[0]
    heads_here = rotated_suffix_keys.shape[1] // HEAD_WIDTH
    group = Q_HEADS // KEY_VALUE_HEADS
    rescale_factor = 1.0 / HEAD_WIDTH**0.5
    owners_here = lax.dynamic_slice_in_dim(owner, lax.axis_index("tp") * heads_here, heads_here, 0)
    query_matrix = queries.reshape(suffix_rows, heads_here, group, HEAD_WIDTH)
    causal_mask = jnp.arange(suffix_rows)[None, :] <= jnp.arange(suffix_rows)[:, None]
    running_state = (
        jnp.full((heads_here, group, suffix_rows), -1e30, jnp.float32),
        jnp.zeros((heads_here, group, suffix_rows), jnp.float32),
        jnp.zeros((heads_here, group, suffix_rows, HEAD_WIDTH), jnp.float32),
    )
    running_state = combine_partials(
        running_state,
        *block_partials(
            query_matrix, rotated_suffix_keys, suffix_values, causal_mask, rescale_factor
        )
    )
    prompt_rows = prefix_keys.shape[0]
    block_count = prompt_rows // BLOCK
    key_piece = from_root(prefix_keys, "rep", owners_here[0])
    value_piece = from_root(prefix_values, "rep", owners_here[0])

    def step_whole(block_index, state):
        begin = block_index * BLOCK
        key_rows = lax.dynamic_slice_in_dim(key_piece, begin, BLOCK, 0)
        value_rows = lax.dynamic_slice_in_dim(value_piece, begin, BLOCK, 0)
        return combine_partials(
            state, *block_partials(query_matrix, key_rows, value_rows, None, rescale_factor)
        )

    running_state = lax.fori_loop(0, block_count, step_whole, running_state)
    output = running_state[2] / running_state[1][..., None]
    head_major = (
        jnp.transpose(output, (2, 0, 1, 3))
        .reshape(suffix_rows, heads_here * group * HEAD_WIDTH)
        .astype(jnp.bfloat16)
    )
    return lax.all_to_all(head_major, "tp", split_axis=0, concat_axis=1, tiled=True)


def solution(mesh):
    in_specs = (P(), P("rep", "tp"), P("rep", "tp"), P("rep", "tp"), P("rep", "tp"), P("rep", "tp"))
    out_specs = P(("rep", "tp"), None)
    return jax.shard_map(local, mesh=mesh, in_specs=in_specs, out_specs=out_specs, check_vma=False)
```

profile of v0, /device:TPU:1, one launch (start us, length us, event | category | flops | bytes accessed | tf_op | source)
XLA Modules:
  0.0 526.9 jit_solution(6265440442665516088)
XLA Ops:
  6.5 0.0 copy-start
  6.5 0.0 all-reduce.3.cloned.1.call-start
  6.5 1.3 dynamic_slice.17
  8.5 1.5 broadcast_select_fusion
  9.9 0.0 copy-start.1
  9.9 0.0 all-reduce.3.cloned.1.call-update
  9.9 1.0 copy-done.1
  11.0 0.2 copy.19
  11.2 0.3 copy.20
  11.5 0.0 copy-done
  11.5 0.0 copy-start.2
  11.5 0.5 fusion.27
  12.0 0.4 convert_reduce_fusion.1
  12.5 0.0 copy-done.2
  12.5 1.2 fusion.29
  13.6 447.6 %all-reduce.3.cloned.1.call-done = (bf16[4096,128]{1,0:T(8,128)(2,1)}, bf16[4096,128]{1,0:T(8,128)(2,1)}) async-done(((bf16[4096,128]{1,0:T(8,128)(2,1)}, bf16[4096,128]{1,0:T(8,128)(2,1)}), (bf16[4096,128]{1,0:T(8,128)(2,1)}, bf16[4096,128]{1,0:T(8,128)(2,1)})) %all-reduce.3.cloned.1.call-update) | async-done | bytes 2097168 | tf_op jit(solution)/shard_map/psum | solution.py:14
  461.3 40.3 %while.17 = (s32[]{:T(128)}, f32[1,8,256]{2,1,0:T(8,128)S(1)}, f32[1,8,256]{2,1,0:T(8,128)S(1)}, f32[1,8,256,128]{3,2,1,0:T(8,128)S(1)}, bf16[4096,128]{1,0:T(8,...) while((s32[]{:T(128)}, f32[1,8,256]{2,1,0:T(8,128)S(1)}, ...), condition=%wide.region_7.8_spmd, body=%wide.region_4.7_spmd.sunk | while | flops 548153344 | bytes 15622307 | solution.py:81
  461.3 1.6 bitcast_reduce_fusion.2
  462.9 0.7 convert_reduce_fusion.3
  463.6 2.6 fusion.52
  466.3 1.6 bitcast_reduce_fusion.2
  467.9 0.7 convert_reduce_fusion.3
  468.7 2.6 fusion.52
  471.3 1.6 bitcast_reduce_fusion.2
  473.0 0.7 convert_reduce_fusion.3
  473.7 2.6 fusion.52
  476.4 1.6 bitcast_reduce_fusion.2
  478.0 0.7 convert_reduce_fusion.3
  478.8 2.6 fusion.52
  481.4 1.6 bitcast_reduce_fusion.2
  483.1 0.7 convert_reduce_fusion.3
  483.8 2.6 fusion.52
  486.5 1.6 bitcast_reduce_fusion.2
  488.1 0.7 convert_reduce_fusion.3
  488.8 2.6 fusion.52
  491.5 1.6 bitcast_reduce_fusion.2
  493.1 0.7 convert_reduce_fusion.3
  493.9 2.6 fusion.52
  496.5 1.6 bitcast_reduce_fusion.2
  498.2 0.7 convert_reduce_fusion.3
  498.9 2.6 fusion.52
  501.6 0.3 fusion.34
  501.9 0.3 copy.21
  502.3 0.2 convert_element_type.34
  502.5 16.7 %all_to_all.16 = bf16[8,32,1024]{2,1,0:T(8,128)(2,1)S(1)} all-to-all(bf16[8,32,1024]{2,1,0:T(8,128)(2,1)S(1)} %convert_element_type.34), channel_id=1, replica_groups=mesh['rep'=64,'tp'=8] {'tp'}, dimensions={0} | all-to-all | bytes 1048576 | tf_op jit(solution)/shard_map/all_to_all | solution.py:88
  519.2 0.8 copy.26
  (27 shorter events, 0.2 us)
Async XLA Ops:
  6.5 4.9 copy-start
  6.5 454.7 %all-reduce.3.cloned.1.call-start = ((), (), s32[]{:S(2)}) async-start(), calls=%async_computation.1 | async-start | bytes 4194304 | tf_op jit(solution)/shard_map/psum | solution.py:14
  9.9 1.0 copy-start.1
  11.5 1.0 copy-start.2
Sparse Core Ops, SparseCore 0:
  10.3 450.9 all-reduce.2
where the time goes:
time: 527 us
  waiting for transfers between devices  448 us (85%)
  matrix products  35.7 us (7%)
  blocking collectives  16.7 us (3%)
  between operations  14.2 us (3%)
  other arithmetic  8.03 us (2%)
    psum x1, waiting for transfers between devices, from_root(): return lax.psum(block, axis)  448 us
    dot_general x9, matrix products, block_partials(): jnp.einsum('kgin,nkd->kgid', weights, value_split, preferred_element_type...  22.2 us
    all_to_all x1, blocking collectives, local(): lax.all_to_all(head_major, 'tp', split_axis=0, concat_axis=1, tiled=True)  16.7 us
    dot_general x9, matrix products, block_partials(): jnp.einsum('ikgd,nkd->kgin', query_matrix, key_split, preferred_element_t...  13.4 us
  transfers between devices with their start and end apart: 1, of which 1 were waited for; matrix products, arithmetic and copies ran while one was open for 0% of the time, Pallas kernels for 0%

commit v1 on v0

v1 whole, which is shorter than its diff:
```python
import functools
import math

import jax
import jax.numpy as jnp
from jax import lax
from jax.experimental import pallas as pl
from jax.experimental.pallas import tpu as pltpu
from jax.sharding import PartitionSpec as P

Q_HEADS = 64
KEY_VALUE_HEADS = 8
GROUP = Q_HEADS // KEY_VALUE_HEADS
WIDTH = 128
PIECE = 64
SCORE_SCALE = math.log2(math.e) / math.sqrt(WIDTH)
NEGATIVE = -1e30
LARGE = 1e30
HEADS_STEP = 2
NT = (((1,), (1,)), ((), ()))
f32, bf16 = jnp.float32, jnp.bfloat16


def with_ones(values):
    return jnp.concatenate([values, jnp.ones(values.shape, values.dtype)], axis=1)


def spread(column, count):
    return jnp.concatenate([column] * count, axis=1)


def flat(kv, part):
    return kv[:, part].reshape(kv.shape[0] * kv.shape[2], WIDTH)


def suffix_scores(query, keys):
    scores = lax.dot_general(query, keys, NT, preferred_element_type=f32) * SCORE_SCALE
    row = lax.broadcasted_iota(jnp.int32, scores.shape, 0)
    col = lax.broadcasted_iota(jnp.int32, scores.shape, 1)
    return jnp.where(col <= row, scores, NEGATIVE)


def add_piece(query, shift, kv_ref, total, tile):
    keys, values = flat(kv_ref, 0), with_ones(flat(kv_ref, 1))
    wide = spread(shift, tile // WIDTH)
    for start in range(0, keys.shape[0], tile):
        scores = lax.dot_general(query, keys[start:start + tile], NT, preferred_element_type=f32)
        weights = jnp.exp2(scores * SCORE_SCALE - wide).astype(bf16)
        total = total + jnp.dot(weights, values[start:start + tile], preferred_element_type=f32)
    return total


def first_kernel(q_ref, k_ref, v_ref, kv_ref, shift_ref, total_ref):
    for head in range(HEADS_STEP):
        query = q_ref[:, head * WIDTH:(head + 1) * WIDTH]
        scores = suffix_scores(query, k_ref[...])
        largest = jnp.max(scores, axis=1, keepdims=True)
        shift = jnp.broadcast_to(largest, (scores.shape[0], WIDTH))
        weights = jnp.exp2(scores - spread(shift, scores.shape[1] // WIDTH)).astype(bf16)
        total = jnp.dot(weights, with_ones(v_ref[...]), preferred_element_type=f32)
        shift_ref[head] = shift
        total_ref[head] = add_piece(query, shift, kv_ref, total, 512)


def next_kernel(q_ref, shift_ref, total_in, kv_ref, total_ref):
    for head in range(HEADS_STEP):
        query = q_ref[:, head * WIDTH:(head + 1) * WIDTH]
        total_ref[head] = add_piece(query, shift_ref[head], kv_ref, total_in[head], 512)


def last_kernel(q_ref, shift_ref, total_in, kv_ref, k_ref, v_ref, a_ref, b_ref, c_ref, out_ref):
    worst = []
    for head in range(HEADS_STEP):
        query = q_ref[:, head * WIDTH:(head + 1) * WIDTH]
        total = add_piece(query, shift_ref[head], kv_ref, total_in[head], 512)
        weight = total[:, WIDTH:]
        worst.append(jnp.where(weight < LARGE, 0.0, 1.0))
        out_ref[:, head * WIDTH:(head + 1) * WIDTH] = (total[:, :WIDTH] / weight).astype(bf16)

    @pl.when(jnp.max(sum(worst)) > 0.0)
    def _():
        for head in range(HEADS_STEP):
            query = q_ref[:, head * WIDTH:(head + 1) * WIDTH]
            state = (jnp.full((query.shape[0], 1), NEGATIVE, f32), jnp.zeros((query.shape[0], 2 * WIDTH), f32))

            def block(state, scores, values):
                shift, total = state
                newest = jnp.maximum(shift, jnp.max(scores, axis=1, keepdims=True))
                weights = jnp.exp2(scores - newest).astype(bf16)
                added = jnp.dot(weights, with_ones(values), preferred_element_type=f32)
                return newest, total * jnp.exp2(shift - newest) + added

            state = block(state, suffix_scores(query, k_ref[...]), v_ref[...])
            for ref in (a_ref, b_ref, c_ref, kv_ref):
                def step(i, state, ref=ref):
                    at = pl.ds(i * 4, 4)
                    keys = ref[at, 0].reshape(4 * PIECE, WIDTH)
                    values = ref[at, 1].reshape(4 * PIECE, WIDTH)
                    scores = lax.dot_general(query, keys, NT, preferred_element_type=f32) * SCORE_SCALE
                    return block(state, scores, values)
                state = lax.fori_loop(0, ref.shape[0] // 4, step, state)
            total = state[1]
            out_ref[:, head * WIDTH:(head + 1) * WIDTH] = (total[:, :WIDTH] / total[:, WIDTH:]).astype(bf16)


def whole(array):
    return pl.BlockSpec(array.shape, lambda i: (0,) * array.ndim)


def call(kernel, queries, others, out_shapes, out_specs, specs, keys):
    flops = 4 * queries.shape[0] * GROUP * keys * WIDTH
    return pl.pallas_call(
        kernel,
        grid=(GROUP // HEADS_STEP,),
        in_specs=[pl.BlockSpec((queries.shape[0], HEADS_STEP * WIDTH), lambda i: (0, i))] + specs,
        out_specs=out_specs,
        out_shape=out_shapes,
        compiler_params=pltpu.CompilerParams(vmem_limit_bytes=48 * 1024 * 1024),
        cost_estimate=pl.CostEstimate(flops=3 * flops, bytes_accessed=4 * 1024 * 1024, transcendentals=0),
    )(queries, *others)


def local(owner, queries, rotated_suffix_keys, suffix_values, prefix_keys, prefix_values):
    rep, tp = lax.axis_index("rep"), lax.axis_index("tp")
    size = lax.axis_size("rep")
    rows = queries.shape[0]
    mine = owner[tp]
    core, side = rep % 2, (rep // 2) % 2
    owner_core, owner_side, owner_z = mine % 2, (mine // 2) % 2, mine // 4
    swap_core = [(i, i ^ 1) for i in range(size)]
    swap_side = [(i, i ^ 2) for i in range(size)]
    along_z = [list(range(start, size, 4)) for start in range(4)]

    slot = jnp.concatenate(
        [prefix_keys.reshape(size, 1, PIECE, WIDTH), prefix_values.reshape(size, 1, PIECE, WIDTH)], axis=1
    )

    def halve(array, at, owner_at, swap):
        half = array.shape[0] // 2
        kept = lax.dynamic_slice_in_dim(array, at * half, half, 0)
        sent = lax.dynamic_slice_in_dim(array, (1 - at) * half, half, 0)
        got = lax.ppermute(sent, "rep", swap)
        return jnp.where(owner_at == at, kept, got)

    part = halve(slot, core, owner_core, swap_core)
    part = halve(part, side, owner_side, swap_side)
    part = lax.all_to_all(part, "rep", 0, 0, axis_index_groups=along_z, tiled=True)
    part = lax.dynamic_slice_in_dim(part, owner_z, 1, 0)
    own = lax.all_gather(part, "rep", axis_index_groups=along_z, tiled=True)

    from_side = lax.ppermute(own, "rep", swap_side)
    from_core = lax.ppermute(own, "rep", swap_core)
    from_both = lax.ppermute(from_side, "rep", swap_core)

    piece = own.shape[0] * PIECE
    shift_shape = jax.ShapeDtypeStruct((GROUP, rows, WIDTH), f32)
    total_shape = jax.ShapeDtypeStruct((GROUP, rows, 2 * WIDTH), f32)
    shift_spec = pl.BlockSpec((HEADS_STEP, rows, WIDTH), lambda i: (i, 0, 0))
    total_spec = pl.BlockSpec((HEADS_STEP, rows, 2 * WIDTH), lambda i: (i, 0, 0))
    suffix = (rotated_suffix_keys, suffix_values)
    shift, total = call(
        first_kernel, queries, (*suffix, own), (shift_shape, total_shape), (shift_spec, total_spec),
        [whole(suffix[0]), whole(suffix[1]), whole(own)], piece + rows,
    )
    for more in (from_core, from_side):
        total = call(
            next_kernel, queries, (shift, total, more), total_shape, total_spec,
            [shift_spec, total_spec, whole(more)], piece,
        )
    output = call(
        last_kernel, queries, (shift, total, from_both, *suffix, own, from_core, from_side),
        jax.ShapeDtypeStruct(queries.shape, bf16),
        pl.BlockSpec((rows, HEADS_STEP * WIDTH), lambda i: (0, i)),
        [shift_spec, total_spec, whole(from_both), whole(suffix[0]), whole(suffix[1]), whole(own), whole(own), whole(own)],
        piece,
    )
    return lax.all_to_all(output, "tp", split_axis=0, concat_axis=1, tiled=True)


def solution(mesh):
    in_specs = (P(), P("rep", "tp"), P("rep", "tp"), P("rep", "tp"), P("rep", "tp"), P("rep", "tp"))
    out_specs = P(("rep", "tp"), None)
    return jax.shard_map(local, mesh=mesh, in_specs=in_specs, out_specs=out_specs, check_vma=False)
```

time: 527 us -> 152 us (0.29)
  waiting for transfers between devices: 448 us -> 36.1 us
  starting transfers between devices: 0.01 us -> 38.5 us
  matrix products: 35.7 us -> 0 us
  blocking collectives: 16.7 us -> 46.2 us
  Pallas kernels: 0 us -> 18.7 us
  between operations: 14.2 us -> 2.96 us
    psum x1 -> x0, waiting for transfers between devices: 448 us -> none  [from_root(): return lax.psum(block, axis)]
    dot_general x18 -> x0, matrix products: 35.7 us -> none  [the longest x9 22.2 us: block_partials(): jnp.einsum('kgin,nkd->kgid', weights, value_split, preferred_element_type...]
    ppermute x0 -> x5, starting transfers between devices: none -> 28.9 us  [the longest x1 12.9 us: local(): from_core = lax.ppermute(own, 'rep', swap_core)]
    all_gather x0 -> x1, blocking collectives: none -> 28.6 us  [local(): own = lax.all_gather(part, 'rep', axis_index_groups=along_z, tiled=True)]
    all_to_all x0 -> x1, waiting for transfers between devices: none -> 23.8 us  [local(): lax.all_to_all(part, 'rep', 0, 0, axis_index_groups=along_z, tiled=True)]
    pallas_call x0 -> x4, Pallas kernels: none -> 18.7 us  [call(): pl.pallas_call(kernel, grid=(GROUP // HEADS_STEP,), in_specs=[pl.BlockSpe...]
    ppermute x0 -> x5, waiting for transfers between devices: none -> 12.3 us  [the longest x2 12.3 us: halve(): got = lax.ppermute(sent, 'rep', swap)]
    all_to_all x0 -> x1, starting transfers between devices: none -> 9.58 us  [local(): lax.all_to_all(part, 'rep', 0, 0, axis_index_groups=along_z, tiled=True)]
  transfers between devices with their start and end apart: 1 -> 6, of which waited for: 1 -> 2; matrix products, arithmetic and copies ran while one was open for 0% -> 0% of each run, Pallas kernels for 0% -> 9%
where the time goes in v1:
time: 152 us
  blocking collectives  46.2 us (30%)
  starting transfers between devices  38.5 us (25%)
  waiting for transfers between devices  36.1 us (24%)
  Pallas kernels  18.7 us (12%)
  local copies, waits for them, and re-layouts  5.47 us (4%)
  other arithmetic  3.67 us (2%)
  between operations  2.96 us (2%)
    all_gather x1, blocking collectives, local(): own = lax.all_gather(part, 'rep', axis_index_groups=along_z, tiled=True)  28.6 us
    all_to_all x1, waiting for transfers between devices, local(): lax.all_to_all(part, 'rep', 0, 0, axis_index_groups=along_z, tiled=True)  23.8 us
    pallas_call x4, Pallas kernels, call(): pl.pallas_call(kernel, grid=(GROUP // HEADS_STEP,), in_specs=[pl.BlockSpe...  18.7 us
    all_to_all x1, blocking collectives, local(): return lax.all_to_all(output, 'tp', split_axis=0, concat_axis=1, tiled=True)  17.7 us
    ppermute x1, starting transfers between devices, local(): from_core = lax.ppermute(own, 'rep', swap_core)  12.9 us
    ppermute x2, waiting for transfers between devices, halve(): got = lax.ppermute(sent, 'rep', swap)  12.3 us
    ppermute x2, starting transfers between devices, halve(): got = lax.ppermute(sent, 'rep', swap)  10.8 us
    all_to_all x1, starting transfers between devices, local(): lax.all_to_all(part, 'rep', 0, 0, axis_index_groups=along_z, tiled=True)  9.58 us
  transfers between devices with their start and end apart: 6, of which 2 were waited for; matrix products, arithmetic and copies ran while one was open for 0% of the time, Pallas kernels for 9%

profile of v1, /device:TPU:1, one launch (start us, length us, event | category | flops | bytes accessed | tf_op | source)
XLA Modules:
  0.0 151.6 jit_solution(996615371955097265)
XLA Ops:
  0.0 0.0 copy-start.6
  0.0 0.0 copy-start.7
  0.0 0.0 copy-start.8
  0.0 1.4 fusion
  1.5 8.8 %collective-permute-start = (bf16[32,2,64,128]{3,2,1,0:T(8,128)(2,1)S(1)}, bf16[32,2,64,128]{3,2,1,0:T(8,128)(2,1)}, u32[]{:S(2)}, u32[]{:S(2)}) collective-permute-start(bf16[32,2,64,128]{3,2,1,0:T(8,128)(2,1)S(1)} %fusion), channel_id=1, source_target_pairs={{0,8},{8,0},{16,24},{24,16},{32,40},{40,32},{48,56},{56,48},{64,72... | collective-permute-start | bytes 3145736 | tf_op jit(solution)/shard_map/ppermute | solution.py:142
  10.3 0.0 copy-done.8
  10.3 0.6 dynamic_slice.18
  12.9 0.0 collective-permute-done
  12.9 0.0 copy-done.6
  12.9 0.0 copy-done.7
  12.9 1.4 fusion.2
  14.3 0.0 copy-start
  14.3 0.0 copy-start.1
  14.3 0.0 copy-start.2
  14.4 2.1 %collective-permute-start.1 = (bf16[16,2,64,128]{3,2,1,0:T(8,128)(2,1)S(1)}, bf16[16,2,64,128]{3,2,1,0:T(8,128)(2,1)S(1)}, u32[]{:S(2)}, u32[]{:S(2)}) collective-permute-start(bf16[16,2,64,128]{3,2,1,0:T(8,128)(2,1)S(1)} %constant_dynamic-slice_fusion.1), channel_id=1, source_target_pairs={{0,16},{8,24},{16,0},{24,8},{32,48},{40,56},{48,32},{56,40},{64,80... | collective-permute-start | bytes 1572872 | tf_op jit(solution)/shard_map/ppermute | solution.py:142
  17.1 12.3 %collective-permute-done.1 = bf16[16,2,64,128]{3,2,1,0:T(8,128)(2,1)S(1)} collective-permute-done((bf16[16,2,64,128]{3,2,1,0:T(8,128)(2,1)S(1)}, bf16[16,2,64,128]{3,2,1,0:T(8,128)(2,1)S(1)}, u32[]{:S(2)}, u32[]{:S(2)}) %collective-permute-start.1) | collective-permute-done | bytes 524320 | tf_op jit(solution)/shard_map/ppermute | solution.py:142
  29.4 0.8 dynamic-slice_select_fusion
  30.3 9.6 %all-to-all-start = ((bf16[16,2,64,128]{3,2,1,0:T(8,128)(2,1)}), bf16[16,2,64,128]{3,2,1,0:T(8,128)(2,1)S(1)}, u32[]{:S(2)}, u32[]{:S(2)}) async-start(bf16[16,2,64,128]{3,2,1,0:T(8,128)(2,1)} %dynamic-slice_select_fusion), calls=%async_computation | async-start | bytes 1048576 | tf_op jit(solution)/shard_map/all_to_all | solution.py:147
  39.9 23.8 %all-to-all-done = bf16[16,2,64,128]{3,2,1,0:T(8,128)(2,1)S(1)} async-done(((bf16[16,2,64,128]{3,2,1,0:T(8,128)(2,1)}), bf16[16,2,64,128]{3,2,1,0:T(8,128)(2,1)S(1)}, u32[]{:S(2)}, u32[]{:S(2)}) %all-to-all-start) | async-done | bytes 524320 | tf_op jit(solution)/shard_map/all_to_all | solution.py:147
  63.7 28.6 %all_gather.3.kv_ref.a_ref = bf16[16,2,64,128]{3,2,1,0:T(8,128)(2,1)S(1)} all-gather(bf16[1,2,64,128]{3,2,1,0:T(8,128)(2,1)S(1)} %constant_dynamic-slice_fusion), channel_id=1, replica_groups={{0,32,64,96,128,160,192,224,256,288,320,352,384,416,448,480},{8,40,72,1..., dimensions={0}, use_global_device_ids=true | all-gather | bytes 557056 | tf_op jit(solution)/shard_map/all_gather | solution.py:149
  92.2 3.1 %collective-permute-start.3 = (bf16[16,2,64,128]{3,2,1,0:T(8,128)(2,1)S(1)}, bf16[16,2,64,128]{3,2,1,0:T(8,128)(2,1)S(1)}, u32[]{:S(2)}, u32[]{:S(2)}) collective-permute-start(bf16[16,2,64,128]{3,2,1,0:T(8,128)(2,1)S(1)} %all_gather.3.kv_ref.a_ref), channel_id=1, source_target_pairs={{0,16},{8,24},{16,0},{24,8},{32,48},{40,56},{48,32},{56,40},{64,80... | collective-permute-start | bytes 1572872 | tf_op jit(solution)/shard_map/ppermute | solution.py:151
  95.3 12.9 %collective-permute-start.2 = (bf16[16,2,64,128]{3,2,1,0:T(8,128)(2,1)S(1)}, bf16[16,2,64,128]{3,2,1,0:T(8,128)(2,1)S(1)}, u32[]{:S(2)}, u32[]{:S(2)}) collective-permute-start(bf16[16,2,64,128]{3,2,1,0:T(8,128)(2,1)S(1)} %all_gather.3.kv_ref.a_ref), channel_id=1, source_target_pairs={{0,8},{8,0},{16,24},{24,16},{32,40},{40,32},{48,56},{56,48},{64,72... | collective-permute-start | bytes 1572872 | tf_op jit(solution)/shard_map/ppermute | solution.py:152
  108.3 0.0 copy-done
  108.3 0.0 copy-done.1
  108.3 0.0 copy-done.2
  108.3 4.2 %shard_map.64 = (f32[8,256,128]{2,1,0:T(8,128)S(1)}, f32[8,256,256]{2,1,0:T(8,128)S(1)}) custom-call(bf16[256,1024]{1,0:T(8,128)(2,1)S(1)} %copy-done, bf16[256,128]{1,0:T(8,128)(2,1)S(1)} %copy-done.1, bf16[256,128]{1,0:T(8,128)(2,1)S(1)} %copy-done.2, bf16[16,2,64,128]{3,2,1,0:T(8,128)(2,1)S(1)} %all_gather.3.kv_ref.a_ref), custom_call_target="tpu_custom_call" | custom-call | flops 4026531840 | bytes 4194304 | tf_op jit(solution)/shard_map/pallas_call | solution.py:112
  112.6 0.0 copy-start.4
  112.6 1.3 copy-done.4
  113.9 0.0 collective-permute-done.3.kv_ref.c_ref
  113.9 2.0 %collective-permute-start.4 = (bf16[16,2,64,128]{3,2,1,0:T(8,128)(2,1)S(1)}, bf16[16,2,64,128]{3,2,1,0:T(8,128)(2,1)S(1)}, u32[]{:S(2)}, u32[]{:S(2)}) collective-permute-start(bf16[16,2,64,128]{3,2,1,0:T(8,128)(2,1)S(1)} %collective-permute-done.3.kv_ref.c_ref), channel_id=1, source_target_pairs={{0,8},{8,0},{16,24},{24,16},{32,40},{40,32},{48,56},{56,48},{64,72... | collective-permute-start | bytes 1572872 | tf_op jit(solution)/shard_map/ppermute | solution.py:153
  115.9 0.0 collective-permute-done.2.kv_ref.b_ref
  116.0 4.7 %shard_map.65.total_in = f32[8,256,256]{2,1,0:T(8,128)S(1)} custom-call(bf16[256,1024]{1,0:T(8,128)(2,1)S(1)} %copy-done, f32[8,256,128]{2,1,0:T(8,128)S(1)} %get-tuple-element.7.shift_ref, f32[8,256,256]{2,1,0:T(8,128)} %copy-done.4, bf16[16,2,64,128]{3,2,1,0:T(8,128)(2,1)S(1)} %collective-permute-done.2.kv_ref.b_ref), custom_call_target="tpu_custom_call" | custom-call | flops 3221225472 | bytes 4194304 | tf_op jit(solution)/shard_map/pallas_call | solution.py:112
  120.7 0.0 copy-start.5
  120.7 1.3 copy-done.5
  122.0 4.7 %shard_map.66.total_in = f32[8,256,256]{2,1,0:T(8,128)S(1)} custom-call(bf16[256,1024]{1,0:T(8,128)(2,1)S(1)} %copy-done, f32[8,256,128]{2,1,0:T(8,128)S(1)} %get-tuple-element.7.shift_ref, f32[8,256,256]{2,1,0:T(8,128)} %copy-done.5, bf16[16,2,64,128]{3,2,1,0:T(8,128)(2,1)S(1)} %collective-permute-done.3.kv_ref.c_ref), custom_call_target="tpu_custom_call" | custom-call | flops 3221225472 | bytes 4194304 | tf_op jit(solution)/shard_map/pallas_call | solution.py:112
  126.7 0.0 copy-start.3
  126.7 1.3 copy-done.3
  128.0 0.0 collective-permute-done.4.kv_ref
  128.0 5.1 %shard_map.67 = bf16[256,1024]{1,0:T(8,128)(2,1)S(1)} custom-call(bf16[256,1024]{1,0:T(8,128)(2,1)S(1)} %copy-done, f32[8,256,128]{2,1,0:T(8,128)S(1)} %get-tuple-element.7.shift_ref, f32[8,256,256]{2,1,0:T(8,128)} %copy-done.3, bf16[16,2,64,128]{3,2,1,0:T(8,128)(2,1)S(1)} %collective-permute-done.4.kv_ref, bf16[256,128]{1,0:T(8,128)(2,1)S(1)} %copy-done.1, ...), custom_call_target="tpu_custom_call" | custom-call | flops 3221225472 | bytes 4194304 | tf_op jit(solution)/shard_map/pallas_call | solution.py:112
  133.1 17.7 %all_to_all.24 = bf16[8,32,1024]{2,1,0:T(8,128)(2,1)S(1)} all-to-all(bf16[8,32,1024]{2,1,0:T(8,128)(2,1)S(1)} %bitcast.7), channel_id=1, replica_groups=mesh['rep'=64,'tp'=8] {'tp'}, dimensions={0} | all-to-all | bytes 1048576 | tf_op jit(solution)/shard_map/all_to_all | solution.py:177
  150.8 0.8 copy.9
  (2 shorter events, 0.1 us)
Async XLA Ops:
  0.0 12.9 %copy-start.6 = (bf16[4096,128]{1,0:T(8,128)(2,1)S(1)}, bf16[4096,128]{1,0:T(8,128)(2,1)}, u32[]{:S(2)}) copy-start(bf16[4096,128]{1,0:T(8,128)(2,1)} %param.10) | copy-start | bytes 3145732
  0.0 12.9 %copy-start.7 = (bf16[4096,128]{1,0:T(8,128)(2,1)S(1)}, bf16[4096,128]{1,0:T(8,128)(2,1)}, u32[]{:S(2)}) copy-start(bf16[4096,128]{1,0:T(8,128)(2,1)} %param.11) | copy-start | bytes 3145732
  0.0 10.3 %copy-start.8 = (s32[8]{0:T(128)S(1)}, s32[8]{0:T(128)}, u32[]{:S(2)}) copy-start(s32[8]{0:T(128)} %param.6) | copy-start | bytes 100
  1.5 11.4 %collective-permute-start = (bf16[32,2,64,128]{3,2,1,0:T(8,128)(2,1)S(1)}, bf16[32,2,64,128]{3,2,1,0:T(8,128)(2,1)}, u32[]{:S(2)}, u32[]{:S(2)}) collective-permute-start(bf16[32,2,64,128]{3,2,1,0:T(8,128)(2,1)S(1)} %fusion), channel_id=1, source_target_pairs={{0,8},{8,0},{16,24},{24,16},{32,40},{40,32},{48,56},{56,48},{64,72... | collective-permute-start | bytes 3145736 | tf_op jit(solution)/shard_map/ppermute | solution.py:142
  14.3 94.0 %copy-start = (bf16[256,1024]{1,0:T(8,128)(2,1)S(1)}, bf16[256,1024]{1,0:T(8,128)(2,1)}, u32[]{:S(2)}) copy-start(bf16[256,1024]{1,0:T(8,128)(2,1)} %q_ref.7) | copy-start | bytes 1572868
  14.3 94.0 %copy-start.1 = (bf16[256,128]{1,0:T(8,128)(2,1)S(1)}, bf16[256,128]{1,0:T(8,128)(2,1)}, u32[]{:S(2)}) copy-start(bf16[256,128]{1,0:T(8,128)(2,1)} %k_ref.3) | copy-start | bytes 196612
  14.3 94.0 %copy-start.2 = (bf16[256,128]{1,0:T(8,128)(2,1)S(1)}, bf16[256,128]{1,0:T(8,128)(2,1)}, u32[]{:S(2)}) copy-start(bf16[256,128]{1,0:T(8,128)(2,1)} %v_ref.3) | copy-start | bytes 196612
  14.4 15.0 %collective-permute-start.1 = (bf16[16,2,64,128]{3,2,1,0:T(8,128)(2,1)S(1)}, bf16[16,2,64,128]{3,2,1,0:T(8,128)(2,1)S(1)}, u32[]{:S(2)}, u32[]{:S(2)}) collective-permute-start(bf16[16,2,64,128]{3,2,1,0:T(8,128)(2,1)S(1)} %constant_dynamic-slice_fusion.1), channel_id=1, source_target_pairs={{0,16},{8,24},{16,0},{24,8},{32,48},{40,56},{48,32},{56,40},{64,80... | collective-permute-start | bytes 1572872 | tf_op jit(solution)/shard_map/ppermute | solution.py:142
  30.3 33.4 %all-to-all-start = ((bf16[16,2,64,128]{3,2,1,0:T(8,128)(2,1)}), bf16[16,2,64,128]{3,2,1,0:T(8,128)(2,1)S(1)}, u32[]{:S(2)}, u32[]{:S(2)}) async-start(bf16[16,2,64,128]{3,2,1,0:T(8,128)(2,1)} %dynamic-slice_select_fusion), calls=%async_computation | async-start | bytes 1048576 | tf_op jit(solution)/shard_map/all_to_all | solution.py:147
  92.2 21.7 %collective-permute-start.3 = (bf16[16,2,64,128]{3,2,1,0:T(8,128)(2,1)S(1)}, bf16[16,2,64,128]{3,2,1,0:T(8,128)(2,1)S(1)}, u32[]{:S(2)}, u32[]{:S(2)}) collective-permute-start(bf16[16,2,64,128]{3,2,1,0:T(8,128)(2,1)S(1)} %all_gather.3.kv_ref.a_ref), channel_id=1, source_target_pairs={{0,16},{8,24},{16,0},{24,8},{32,48},{40,56},{48,32},{56,40},{64,80... | collective-permute-start | bytes 1572872 | tf_op jit(solution)/shard_map/ppermute | solution.py:151
  95.3 20.6 %collective-permute-start.2 = (bf16[16,2,64,128]{3,2,1,0:T(8,128)(2,1)S(1)}, bf16[16,2,64,128]{3,2,1,0:T(8,128)(2,1)S(1)}, u32[]{:S(2)}, u32[]{:S(2)}) collective-permute-start(bf16[16,2,64,128]{3,2,1,0:T(8,128)(2,1)S(1)} %all_gather.3.kv_ref.a_ref), channel_id=1, source_target_pairs={{0,8},{8,0},{16,24},{24,16},{32,40},{40,32},{48,56},{56,48},{64,72... | collective-permute-start | bytes 1572872 | tf_op jit(solution)/shard_map/ppermute | solution.py:152
  112.6 1.3 copy-start.4
  113.9 14.1 %collective-permute-start.4 = (bf16[16,2,64,128]{3,2,1,0:T(8,128)(2,1)S(1)}, bf16[16,2,64,128]{3,2,1,0:T(8,128)(2,1)S(1)}, u32[]{:S(2)}, u32[]{:S(2)}) collective-permute-start(bf16[16,2,64,128]{3,2,1,0:T(8,128)(2,1)S(1)} %collective-permute-done.3.kv_ref.c_ref), channel_id=1, source_target_pairs={{0,8},{8,0},{16,24},{24,16},{32,40},{40,32},{48,56},{56,48},{64,72... | collective-permute-start | bytes 1572872 | tf_op jit(solution)/shard_map/ppermute | solution.py:153
  120.7 1.3 copy-start.5
  126.7 1.3 copy-start.3

commit v2 on v1

v2 whole, which is shorter than its diff:
```python
import functools
import math

import jax
import jax.numpy as jnp
from jax import lax
from jax.experimental import pallas as pl
from jax.experimental.pallas import tpu as pltpu
from jax.sharding import PartitionSpec as P

Q_HEADS = 64
KEY_VALUE_HEADS = 8
GROUP = Q_HEADS // KEY_VALUE_HEADS
WIDTH = 128
PIECE = 64
TILE = 1024
SCORE_SCALE = math.log2(math.e) / math.sqrt(WIDTH)
NEGATIVE = -1e30
LARGE = 1e30
NT = (((1,), (1,)), ((), ()))
f32, bf16 = jnp.float32, jnp.bfloat16


def with_ones(values):
    return jnp.concatenate([values, jnp.ones(values.shape, values.dtype)], axis=1)


def spread(column, count):
    return jnp.concatenate([column] * count, axis=1)


def flat(kv_ref, part):
    return kv_ref[:, part].reshape(kv_ref.shape[0] * kv_ref.shape[2], WIDTH)


def head_of(q_ref, head):
    return q_ref[:, head * WIDTH:(head + 1) * WIDTH]


def suffix_scores(query, keys):
    scores = lax.dot_general(query, keys, NT, preferred_element_type=f32) * SCORE_SCALE
    row = lax.broadcasted_iota(jnp.int32, scores.shape, 0)
    col = lax.broadcasted_iota(jnp.int32, scores.shape, 1)
    return jnp.where(col <= row, scores, NEGATIVE)


def add_piece(query, shift, kv_ref, total):
    keys, values = flat(kv_ref, 0), with_ones(flat(kv_ref, 1))
    wide = spread(shift, TILE // WIDTH)
    for start in range(0, keys.shape[0], TILE):
        scores = lax.dot_general(query, keys[start:start + TILE], NT, preferred_element_type=f32)
        weights = jnp.exp2(scores * SCORE_SCALE - wide).astype(bf16)
        total = total + jnp.dot(weights, values[start:start + TILE], preferred_element_type=f32)
    return total


def suffix_kernel(q_ref, k_ref, v_ref, shift_ref, total_ref):
    for head in range(GROUP):
        scores = suffix_scores(head_of(q_ref, head), k_ref[...])
        shift = jnp.broadcast_to(jnp.max(scores, axis=1, keepdims=True), (scores.shape[0], WIDTH))
        weights = jnp.exp2(scores - spread(shift, scores.shape[1] // WIDTH)).astype(bf16)
        shift_ref[head] = shift
        total_ref[head] = jnp.dot(weights, with_ones(v_ref[...]), preferred_element_type=f32)


def next_kernel(q_ref, shift_ref, total_in, kv_ref, total_ref):
    for head in range(GROUP):
        total_ref[head] = add_piece(head_of(q_ref, head), shift_ref[head], kv_ref, total_in[head])


def last_kernel(q_ref, shift_ref, total_in, kv_ref, k_ref, v_ref, other_ref, out_ref):
    worst = jnp.zeros(shift_ref.shape[1:], f32)
    for head in range(GROUP):
        total = add_piece(head_of(q_ref, head), shift_ref[head], kv_ref, total_in[head])
        weight = total[:, WIDTH:]
        worst = jnp.maximum(worst, jnp.where(weight < LARGE, 0.0, 1.0))
        out_ref[:, head * WIDTH:(head + 1) * WIDTH] = (total[:, :WIDTH] / weight).astype(bf16)

    @pl.when(jnp.max(worst) > 0.0)
    def _():
        def one_head(head, carry):
            at = pl.ds(pl.multiple_of(head * WIDTH, WIDTH), WIDTH)
            query = q_ref[:, at]

            def block(state, scores, values):
                shift, total = state
                newest = jnp.maximum(shift, jnp.max(scores, axis=1, keepdims=True))
                weights = jnp.exp2(scores - newest).astype(bf16)
                added = jnp.dot(weights, with_ones(values), preferred_element_type=f32)
                return newest, total * jnp.exp2(shift - newest) + added

            state = (jnp.full((query.shape[0], 1), NEGATIVE, f32), jnp.zeros((query.shape[0], 2 * WIDTH), f32))
            state = block(state, suffix_scores(query, k_ref[...]), v_ref[...])
            for ref in (other_ref, kv_ref):
                def step(i, state, ref=ref):
                    some = ref.at[pl.ds(i * 8, 8)]
                    scores = lax.dot_general(query, flat(some, 0), NT, preferred_element_type=f32) * SCORE_SCALE
                    return block(state, scores, flat(some, 1))

                state = lax.fori_loop(0, ref.shape[0] // 8, step, state)
            total = state[1]
            out_ref[:, at] = (total[:, :WIDTH] / total[:, WIDTH:]).astype(bf16)
            return carry

        lax.fori_loop(0, GROUP, one_head, 0)


def call(kernel, out_shape, keys, *args):
    flops = 8 * args[0].shape[0] * GROUP * keys * WIDTH
    in_vmem = pl.BlockSpec(memory_space=pltpu.VMEM)
    return pl.pallas_call(
        kernel,
        in_specs=[in_vmem] * len(args),
        out_specs=jax.tree.map(lambda _: in_vmem, out_shape),
        out_shape=out_shape,
        compiler_params=pltpu.CompilerParams(vmem_limit_bytes=24 * 1024 * 1024),
        cost_estimate=pl.CostEstimate(flops=flops, bytes_accessed=4 * 1024 * 1024, transcendentals=0),
    )(*args)


def local(owner, queries, rotated_suffix_keys, suffix_values, prefix_keys, prefix_values):
    rep, tp = lax.axis_index("rep"), lax.axis_index("tp")
    size = lax.axis_size("rep")
    rows = queries.shape[0]
    mine = owner[tp]
    owner_core, owner_side, owner_z = mine % 2, (mine // 2) % 2, mine // 4

    def place(z, side, core):
        return 4 * z + 2 * side + core

    near = [[place(2 * a + b, s, c) for b in range(2) for s in range(2)] for a in range(8) for c in range(2)]
    far = [[place(2 * a + b, s, c) for a in range(8)] for b in range(2) for s in range(2) for c in range(2)]
    swap_core = [(i, i ^ 1) for i in range(size)]

    def exchange(array, groups):
        return lax.all_to_all(array, "rep", 0, 0, axis_index_groups=groups, tiled=True)

    def pick(array, at, count):
        share = array.shape[0] // count
        return lax.dynamic_slice_in_dim(array, at * share, share, 0)

    def copies(array, count):
        many = jnp.broadcast_to(array[None], (count, *array.shape))
        return many.reshape(count * array.shape[0], *array.shape[1:])

    shape = (prefix_keys.shape[0] // PIECE, 1, PIECE, WIDTH)
    slot = jnp.concatenate([prefix_keys.reshape(shape), prefix_values.reshape(shape)], axis=1)
    half = shape[0] // 2
    core = rep % 2
    kept = lax.dynamic_slice_in_dim(slot, core * half, half, 0)
    sent = lax.dynamic_slice_in_dim(slot, (1 - core) * half, half, 0)
    part = jnp.where(owner_core == core, kept, lax.ppermute(sent, "rep", swap_core))
    part = pick(exchange(part, near), (owner_z % 2) * 2 + owner_side, 4)
    part = pick(exchange(part, far), owner_z // 2, 8)
    part = exchange(copies(part, 8), far)
    first = exchange(copies(part, 4), near)
    second = lax.ppermute(first, "rep", swap_core)

    shift_shape = jax.ShapeDtypeStruct((GROUP, rows, WIDTH), f32)
    total_shape = jax.ShapeDtypeStruct((GROUP, rows, 2 * WIDTH), f32)
    suffix = (rotated_suffix_keys, suffix_values)
    shift, total = call(suffix_kernel, (shift_shape, total_shape), rows, queries, *suffix)
    total = call(next_kernel, total_shape, half * PIECE, queries, shift, total, first)
    output = call(
        last_kernel, jax.ShapeDtypeStruct(queries.shape, bf16), half * PIECE,
        queries, shift, total, second, *suffix, first,
    )
    return lax.all_to_all(output, "tp", split_axis=0, concat_axis=1, tiled=True)


def solution(mesh):
    in_specs = (P(), P("rep", "tp"), P("rep", "tp"), P("rep", "tp"), P("rep", "tp"), P("rep", "tp"))
    out_specs = P(("rep", "tp"), None)
    return jax.shard_map(local, mesh=mesh, in_specs=in_specs, out_specs=out_specs, check_vma=False)
```

time: 152 us -> 134 us (0.88)
  blocking collectives: 46.2 us -> 57.3 us
  starting transfers between devices: 38.5 us -> 28 us
  Pallas kernels: 18.7 us -> 10.3 us
  waiting for transfers between devices: 36.1 us -> 29.3 us
  local copies, waits for them, and re-layouts: 5.47 us -> 2.46 us
    all_to_all x0 -> x2, blocking collectives: none -> 39.4 us  [exchange(): lax.all_to_all(array, 'rep', 0, 0, axis_index_groups=groups, tiled=True)]
    all_gather x1 -> x0, blocking collectives: 28.6 us -> none  [local(): own = lax.all_gather(part, 'rep', axis_index_groups=along_z, tiled=True)]
    ppermute x5 -> x2, starting transfers between devices: 28.9 us -> 15 us  [the longest x1 8.76 us: local(): lax.ppermute(sent, 'rep', swap_core)]
    ppermute x5 -> x2, waiting for transfers between devices: 12.3 us -> 0.01 us  [the longest x1 0.01 us: local(): lax.ppermute(sent, 'rep', swap_core)]
    pallas_call x4 -> x3, Pallas kernels: 18.7 us -> 10.3 us  [call(): pl.pallas_call(kernel, in_specs=[in_vmem] * len(args), out_specs=jax.tree...]
    all_to_all x1 -> x2, waiting for transfers between devices: 23.8 us -> 29.3 us  [exchange(): lax.all_to_all(array, 'rep', 0, 0, axis_index_groups=groups, tiled=True)]
    unnamed x18 -> x12, local copies, waits for them, and re-layouts: 4 us -> 0.02 us
    all_to_all x1 -> x2, starting transfers between devices: 9.58 us -> 13 us  [exchange(): lax.all_to_all(array, 'rep', 0, 0, axis_index_groups=groups, tiled=True)]
  transfers between devices with their start and end apart: 6 -> 4, of which waited for: 2 -> 2; matrix products, arithmetic and copies ran while one was open for 0% -> 0% of each run, Pallas kernels for 9% -> 4%
where the time goes in v2:
time: 134 us
  blocking collectives  57.3 us (43%)
  waiting for transfers between devices  29.3 us (22%)
  starting transfers between devices  28 us (21%)
  Pallas kernels  10.3 us (8%)
  other arithmetic  3.54 us (3%)
  between operations  2.85 us (2%)
  local copies, waits for them, and re-layouts  2.46 us (2%)
    all_to_all x2, blocking collectives, exchange(): lax.all_to_all(array, 'rep', 0, 0, axis_index_groups=groups, tiled=True)  39.4 us
    all_to_all x2, waiting for transfers between devices, exchange(): lax.all_to_all(array, 'rep', 0, 0, axis_index_groups=groups, tiled=True)  29.3 us
    all_to_all x1, blocking collectives, local(): return lax.all_to_all(output, 'tp', split_axis=0, concat_axis=1, tiled=True)  17.9 us
    all_to_all x2, starting transfers between devices, exchange(): lax.all_to_all(array, 'rep', 0, 0, axis_index_groups=groups, tiled=True)  13 us
    pallas_call x3, Pallas kernels, call(): pl.pallas_call(kernel, in_specs=[in_vmem] * len(args), out_specs=jax.tree...  10.3 us
    ppermute x1, starting transfers between devices, local(): lax.ppermute(sent, 'rep', swap_core)  8.76 us
    ppermute x1, starting transfers between devices, local(): second = lax.ppermute(first, 'rep', swap_core)  6.27 us
  transfers between devices with their start and end apart: 4, of which 2 were waited for; matrix products, arithmetic and copies ran while one was open for 0% of the time, Pallas kernels for 4%

profile of v2, /device:TPU:1, one launch (start us, length us, event | category | flops | bytes accessed | tf_op | source)
XLA Modules:
  0.0 133.8 jit_solution(12065300871728026228)
XLA Ops:
  0.0 0.0 copy-start.3
  0.0 0.0 copy-start.4
  0.0 0.0 copy-start.5
  0.0 2.4 %fusion = bf16[32,2,64,128]{3,2,1,0:T(8,128)(2,1)} fusion(s32[]{:T(128)S(6)} %select_n.57, bf16[64,1,64,128]{3,2,1,0:T(8,128)(2,1)} %bitcast.11, bf16[64,1,64,128]{3,2,1,0:T(8,128)(2,1)} %bitcast.13), kind=kLoop, calls=%fused_computation.4 | loop fusion | flops 524288 | bytes 3145732 | tf_op jit(solution)/shard_map/concatenate | solution.py:147
  2.4 8.8 %collective-permute-start = (bf16[32,2,64,128]{3,2,1,0:T(8,128)(2,1)}, bf16[32,2,64,128]{3,2,1,0:T(8,128)(2,1)S(1)}, u32[]{:S(2)}, u32[]{:S(2)}) collective-permute-start(bf16[32,2,64,128]{3,2,1,0:T(8,128)(2,1)} %fusion), channel_id=1, source_target_pairs={{0,8},{8,0},{16,24},{24,16},{32,40},{40,32},{48,56},{56,48},{64,72... | collective-permute-start | bytes 3145736 | tf_op jit(solution)/shard_map/ppermute | solution.py:152
  11.2 0.0 copy-done.5
  11.2 0.6 dynamic_slice.15
  13.8 0.0 collective-permute-done
  13.8 0.0 copy-done.3
  13.8 0.0 copy-done.4
  13.8 1.1 fusion.2
  14.9 3.5 %all-to-all-start = ((bf16[32,2,64,128]{3,2,1,0:T(8,128)(2,1)}), bf16[32,2,64,128]{3,2,1,0:T(8,128)(2,1)S(1)}, u32[]{:S(2)}, u32[]{:S(2)}) async-start(bf16[32,2,64,128]{3,2,1,0:T(8,128)(2,1)} %fusion.2), calls=%async_computation | async-start | bytes 2097152 | tf_op jit(solution)/shard_map/all_to_all | solution.py:136
  19.2 12.8 %all-to-all-done = bf16[32,2,64,128]{3,2,1,0:T(8,128)(2,1)S(1)} async-done(((bf16[32,2,64,128]{3,2,1,0:T(8,128)(2,1)}), bf16[32,2,64,128]{3,2,1,0:T(8,128)(2,1)S(1)}, u32[]{:S(2)}, u32[]{:S(2)}) %all-to-all-start) | async-done | bytes 1048608 | tf_op jit(solution)/shard_map/all_to_all | solution.py:136
  31.9 0.7 constant_dynamic-slice_fusion
  32.7 9.4 %all-to-all-start.1 = ((bf16[8,2,64,128]{3,2,1,0:T(8,128)(2,1)}), bf16[8,2,64,128]{3,2,1,0:T(8,128)(2,1)S(1)}, u32[]{:S(2)}, u32[]{:S(2)}) async-start(bf16[8,2,64,128]{3,2,1,0:T(8,128)(2,1)} %constant_dynamic-slice_fusion), calls=%async_computation.1 | async-start | bytes 524288 | tf_op jit(solution)/shard_map/all_to_all | solution.py:136
  42.1 16.5 %all-to-all-done.1 = bf16[8,2,64,128]{3,2,1,0:T(8,128)(2,1)S(1)} async-done(((bf16[8,2,64,128]{3,2,1,0:T(8,128)(2,1)}), bf16[8,2,64,128]{3,2,1,0:T(8,128)(2,1)S(1)}, u32[]{:S(2)}, u32[]{:S(2)}) %all-to-all-start.1) | async-done | bytes 262176 | tf_op jit(solution)/shard_map/all_to_all | solution.py:136
  58.7 0.0 copy-start
  58.7 0.0 copy-start.1
  58.7 0.0 copy-start.2
  58.7 23.0 %all_to_all.39 = bf16[8,2,64,128]{3,2,1,0:T(8,128)(2,1)S(1)} all-to-all(bf16[8,2,64,128]{3,2,1,0:T(8,128)(2,1)S(1)} %reshape.21), channel_id=1, replica_groups={{0,64,128,192,256,320,384,448},{8,72,136,200,264,328,392,456},{16,80,14..., dimensions={0} | all-to-all | bytes 524288 | tf_op jit(solution)/shard_map/all_to_all | solution.py:136
  81.7 0.2 broadcast_in_dim.5
  82.0 16.5 %all_to_all.40.kv_ref.other_ref = bf16[32,2,64,128]{3,2,1,0:T(8,128)(2,1)S(1)} all-to-all(bf16[32,2,64,128]{3,2,1,0:T(8,128)(2,1)S(1)} %bitcast.15), channel_id=1, replica_groups={{0,16,32,48},{8,24,40,56},{64,80,96,112},{72,88,104,120},{128,144,160,1..., dimensions={0} | all-to-all | bytes 2097152 | tf_op jit(solution)/shard_map/all_to_all | solution.py:136
  98.4 6.3 %collective-permute-start.1 = (bf16[32,2,64,128]{3,2,1,0:T(8,128)(2,1)S(1)}, bf16[32,2,64,128]{3,2,1,0:T(8,128)(2,1)S(1)}, u32[]{:S(2)}, u32[]{:S(2)}) collective-permute-start(bf16[32,2,64,128]{3,2,1,0:T(8,128)(2,1)S(1)} %all_to_all.40.kv_ref.other_ref), channel_id=1, source_target_pairs={{0,8},{8,0},{16,24},{24,16},{32,40},{40,32},{48,56},{56,48},{64,72... | collective-permute-start | bytes 3145736 | tf_op jit(solution)/shard_map/ppermute | solution.py:157
  104.7 0.0 copy-done
  104.7 0.0 copy-done.1
  104.7 0.0 copy-done.2
  104.7 0.9 shard_map.64
  105.6 4.6 %shard_map.65.total_in = f32[8,256,256]{2,1,0:T(8,128)S(1)} custom-call(bf16[256,1024]{1,0:T(8,128)(2,1)S(1)} %copy-done, f32[8,256,128]{2,1,0:T(8,128)S(1)} %get-tuple-element.7.shift_ref, f32[8,256,256]{2,1,0:T(8,128)S(1)} %get-tuple-element.8.total_in, bf16[32,2,64,128]{3,2,1,0:T(8,128)(2,1)S(1)} %all_to_all.40.kv_ref.other_ref), custom_call_target="tpu_custom_call" | custom-call | flops 4294967296 | bytes 4194304 | tf_op jit(solution)/shard_map/pallas_call | solution.py:111
  110.3 0.0 collective-permute-done.1.kv_ref
  110.3 4.8 %shard_map.66 = bf16[256,1024]{1,0:T(8,128)(2,1)S(1)} custom-call(bf16[256,1024]{1,0:T(8,128)(2,1)S(1)} %copy-done, f32[8,256,128]{2,1,0:T(8,128)S(1)} %get-tuple-element.7.shift_ref, f32[8,256,256]{2,1,0:T(8,128)S(1)} %shard_map.65.total_in, bf16[32,2,64,128]{3,2,1,0:T(8,128)(2,1)S(1)} %collective-permute-done.1.kv_ref, bf16[256,128]{1,0:T(8,128)(2,1)S(1)} %copy-done.1, ...), custom_call_target="tpu_custom_call" | custom-call | flops 4294967296 | bytes 4194304 | tf_op jit(solution)/shard_map/pallas_call | solution.py:111
  115.1 17.9 %all_to_all.41 = bf16[8,32,1024]{2,1,0:T(8,128)(2,1)S(1)} all-to-all(bf16[8,32,1024]{2,1,0:T(8,128)(2,1)S(1)} %bitcast.10), channel_id=1, replica_groups=mesh['rep'=64,'tp'=8] {'tp'}, dimensions={0} | all-to-all | bytes 1048576 | tf_op jit(solution)/shard_map/all_to_all | solution.py:168
  133.0 0.8 copy.9
  (2 shorter events, 0.0 us)
Async XLA Ops:
  0.0 13.8 %copy-start.3 = (bf16[4096,128]{1,0:T(8,128)(2,1)S(1)}, bf16[4096,128]{1,0:T(8,128)(2,1)}, u32[]{:S(2)}) copy-start(bf16[4096,128]{1,0:T(8,128)(2,1)} %param.10) | copy-start | bytes 3145732
  0.0 13.8 %copy-start.4 = (bf16[4096,128]{1,0:T(8,128)(2,1)S(1)}, bf16[4096,128]{1,0:T(8,128)(2,1)}, u32[]{:S(2)}) copy-start(bf16[4096,128]{1,0:T(8,128)(2,1)} %param.11) | copy-start | bytes 3145732
  0.0 11.2 %copy-start.5 = (s32[8]{0:T(128)S(1)}, s32[8]{0:T(128)}, u32[]{:S(2)}) copy-start(s32[8]{0:T(128)} %param.6) | copy-start | bytes 100
  2.4 11.3 %collective-permute-start = (bf16[32,2,64,128]{3,2,1,0:T(8,128)(2,1)}, bf16[32,2,64,128]{3,2,1,0:T(8,128)(2,1)S(1)}, u32[]{:S(2)}, u32[]{:S(2)}) collective-permute-start(bf16[32,2,64,128]{3,2,1,0:T(8,128)(2,1)} %fusion), channel_id=1, source_target_pairs={{0,8},{8,0},{16,24},{24,16},{32,40},{40,32},{48,56},{56,48},{64,72... | collective-permute-start | bytes 3145736 | tf_op jit(solution)/shard_map/ppermute | solution.py:152
  14.9 17.0 %all-to-all-start = ((bf16[32,2,64,128]{3,2,1,0:T(8,128)(2,1)}), bf16[32,2,64,128]{3,2,1,0:T(8,128)(2,1)S(1)}, u32[]{:S(2)}, u32[]{:S(2)}) async-start(bf16[32,2,64,128]{3,2,1,0:T(8,128)(2,1)} %fusion.2), calls=%async_computation | async-start | bytes 2097152 | tf_op jit(solution)/shard_map/all_to_all | solution.py:136
  32.7 26.0 %all-to-all-start.1 = ((bf16[8,2,64,128]{3,2,1,0:T(8,128)(2,1)}), bf16[8,2,64,128]{3,2,1,0:T(8,128)(2,1)S(1)}, u32[]{:S(2)}, u32[]{:S(2)}) async-start(bf16[8,2,64,128]{3,2,1,0:T(8,128)(2,1)} %constant_dynamic-slice_fusion), calls=%async_computation.1 | async-start | bytes 524288 | tf_op jit(solution)/shard_map/all_to_all | solution.py:136
  58.7 46.0 %copy-start = (bf16[256,1024]{1,0:T(8,128)(2,1)S(1)}, bf16[256,1024]{1,0:T(8,128)(2,1)}, u32[]{:S(2)}) copy-start(bf16[256,1024]{1,0:T(8,128)(2,1)} %q_ref.5) | copy-start | bytes 1572868
  58.7 46.1 %copy-start.1 = (bf16[256,128]{1,0:T(8,128)(2,1)S(1)}, bf16[256,128]{1,0:T(8,128)(2,1)}, u32[]{:S(2)}) copy-start(bf16[256,128]{1,0:T(8,128)(2,1)} %k_ref.3) | copy-start | bytes 196612
  58.7 46.1 %copy-start.2 = (bf16[256,128]{1,0:T(8,128)(2,1)S(1)}, bf16[256,128]{1,0:T(8,128)(2,1)}, u32[]{:S(2)}) copy-start(bf16[256,128]{1,0:T(8,128)(2,1)} %v_ref.3) | copy-start | bytes 196612
  98.4 11.9 %collective-permute-start.1 = (bf16[32,2,64,128]{3,2,1,0:T(8,128)(2,1)S(1)}, bf16[32,2,64,128]{3,2,1,0:T(8,128)(2,1)S(1)}, u32[]{:S(2)}, u32[]{:S(2)}) collective-permute-start(bf16[32,2,64,128]{3,2,1,0:T(8,128)(2,1)S(1)} %all_to_all.40.kv_ref.other_ref), channel_id=1, source_target_pairs={{0,8},{8,0},{16,24},{24,16},{32,40},{40,32},{48,56},{56,48},{64,72... | collective-permute-start | bytes 3145736 | tf_op jit(solution)/shard_map/ppermute | solution.py:157

commit v3 on v2

--- a/solution.py
+++ b/solution.py
@@ -123,7 +123,6 @@
     size = lax.axis_size("rep")
     rows = queries.shape[0]
     mine = owner[tp]
-    owner_core, owner_side, owner_z = mine % 2, (mine // 2) % 2, mine // 4
 
     def place(z, side, core):
         return 4 * z + 2 * side + core
@@ -137,22 +136,34 @@
 
     def pick(array, at, count):
         share = array.shape[0] // count
-        return lax.dynamic_slice_in_dim(array, at * share, share, 0)
+        return lax.dynamic_slice_in_dim(array, at * share, share, 0, allow_negative_indices=False)
 
     def copies(array, count):
         many = jnp.broadcast_to(array[None], (count, *array.shape))
         return many.reshape(count * array.shape[0], *array.shape[1:])
 
-    shape = (prefix_keys.shape[0] // PIECE, 1, PIECE, WIDTH)
-    slot = jnp.concatenate([prefix_keys.reshape(shape), prefix_values.reshape(shape)], axis=1)
-    half = shape[0] // 2
-    core = rep % 2
-    kept = lax.dynamic_slice_in_dim(slot, core * half, half, 0)
-    sent = lax.dynamic_slice_in_dim(slot, (1 - core) * half, half, 0)
-    part = jnp.where(owner_core == core, kept, lax.ppermute(sent, "rep", swap_core))
-    part = pick(exchange(part, near), (owner_z % 2) * 2 + owner_side, 4)
-    part = pick(exchange(part, far), owner_z // 2, 8)
-    part = exchange(copies(part, 8), far)
+    count = prefix_keys.shape[0] // 2
+    half = count // PIECE
+    core = rep & 1
+    shape = (half, 2, PIECE, WIDTH)
+    is_key = lax.broadcasted_iota(jnp.int32, shape, 1) == 0
+
+    def half_of(which):
+        at = which * count
+        keys, values = (
+            lax.dynamic_slice_in_dim(array, at, count, 0, allow_negative_indices=False).reshape(half, 1, PIECE, WIDTH)
+            for array in (prefix_keys, prefix_values)
+        )
+        return jnp.where(is_key, keys, values)
+
+    in_near = (mine >> 1) & 3
+    in_far = mine >> 3
+    owner_core = mine - 8 * in_far - 2 * in_near
+    got = lax.ppermute(half_of(1 - core), "rep", swap_core)
+    part = jnp.where(owner_core == core, half_of(core), got)
+    part = pick(exchange(part, near), in_near, 4)
+    part = jnp.where(in_far == rep >> 3, part, jnp.zeros_like(part)).astype(f32)
+    part = lax.psum(part, "rep", axis_index_groups=far).astype(bf16)
     first = exchange(copies(part, 4), near)
     second = lax.ppermute(first, "rep", swap_core)
 

time: 134 us -> 124 us (0.925)
  waiting for transfers between devices: 29.3 us -> 13.7 us
  blocking collectives: 57.3 us -> 69.9 us
  starting transfers between devices: 28 us -> 23 us
  other arithmetic: 3.54 us -> 1.33 us
    psum x0 -> x1, blocking collectives: none -> 40.9 us  [local(): part = lax.psum(part, 'rep', axis_index_groups=far).astype(bf16)]
    all_to_all x2 -> x1, blocking collectives: 39.4 us -> 11.9 us  [exchange(): lax.all_to_all(array, 'rep', 0, 0, axis_index_groups=groups, tiled=True)]
    all_to_all x2 -> x1, waiting for transfers between devices: 29.3 us -> 13.7 us  [exchange(): lax.all_to_all(array, 'rep', 0, 0, axis_index_groups=groups, tiled=True)]
    all_to_all x2 -> x1, starting transfers between devices: 13 us -> 3.51 us  [exchange(): lax.all_to_all(array, 'rep', 0, 0, axis_index_groups=groups, tiled=True)]
    ppermute x1, starting transfers between devices: 6.27 us -> 10.7 us  [local(): second = lax.ppermute(first, 'rep', swap_core)]
    concatenate x1 -> x0, other arithmetic: 2.42 us -> none  [local(): jnp.concatenate([prefix_keys.reshape(shape), prefix_values.reshape(shape)...]
  transfers between devices with their start and end apart: 4 -> 3, of which waited for: 2 -> 1; matrix products, arithmetic and copies ran while one was open for 0% -> 0% of each run, Pallas kernels for 4% -> 4%
where the time goes in v3:
time: 124 us
  blocking collectives  69.9 us (56%)
  starting transfers between devices  23 us (19%)
  waiting for transfers between devices  13.7 us (11%)
  Pallas kernels  10.3 us (8%)
  local copies, waits for them, and re-layouts  3.34 us (3%)
  between operations  2.12 us (2%)
  other arithmetic  1.33 us (1%)
    psum x1, blocking collectives, local(): part = lax.psum(part, 'rep', axis_index_groups=far).astype(bf16)  40.9 us
    all_to_all x1, blocking collectives, local(): return lax.all_to_all(output, 'tp', split_axis=0, concat_axis=1, tiled=True)  17 us
    all_to_all x1, waiting for transfers between devices, exchange(): lax.all_to_all(array, 'rep', 0, 0, axis_index_groups=groups, tiled=True)  13.7 us
    all_to_all x1, blocking collectives, exchange(): lax.all_to_all(array, 'rep', 0, 0, axis_index_groups=groups, tiled=True)  11.9 us
    ppermute x1, starting transfers between devices, local(): second = lax.ppermute(first, 'rep', swap_core)  10.7 us
    pallas_call x3, Pallas kernels, call(): pl.pallas_call(kernel, in_specs=[in_vmem] * len(args), out_specs=jax.tree...  10.3 us
    ppermute x1, starting transfers between devices, local(): got = lax.ppermute(half_of(1 - core), 'rep', swap_core)  8.79 us
    all_to_all x1, starting transfers between devices, exchange(): lax.all_to_all(array, 'rep', 0, 0, axis_index_groups=groups, tiled=True)  3.51 us
  transfers between devices with their start and end apart: 3, of which 1 were waited for; matrix products, arithmetic and copies ran while one was open for 0% of the time, Pallas kernels for 4%

profile of v3, /device:TPU:1, one launch (start us, length us, event | category | flops | bytes accessed | tf_op | source)
XLA Modules:
  0.0 123.6 jit_solution(11282568524247419953)
XLA Ops:
  0.0 1.7 %constant_dynamic-slice_fusion.2 = (bf16[2048,128]{1,0:T(8,128)(2,1)S(1)}, bf16[2048,128]{1,0:T(8,128)(2,1)S(1)}, bf16[2048,128]{1,0:T(8,128)(2,1)S(1)}, bf16[2048,128]{1,0:T(8,128)(2,1)S(1)}) fusion(bf16[4096,128]{1,0:T(8,128)(2,1)} %param.11, s32[]{:T(128)S(6)} %mul.13, s32[]{:T(128)S(6)} %mul.14, bf16[4096,128]{1,0:T(8,128)(2,1)} %param.10), kind=kLoop, calls=%fused_computation.5 | loop fusion | bytes 4194312 | tf_op jit(solution)/shard_map/dynamic_slice | solution.py:154
  1.7 0.0 copy-start.3
  1.7 0.1 broadcast_select_fusion
  1.8 8.8 %collective-permute-start = (bf16[32,2,64,128]{3,2,1,0:T(8,128)(2,1)S(1)}, bf16[32,2,64,128]{3,2,1,0:T(8,128)(2,1)S(1)}, u32[]{:S(2)}, u32[]{:S(2)}) collective-permute-start(bf16[32,2,64,128]{3,2,1,0:T(8,128)(2,1)S(1)} %broadcast_select_fusion), channel_id=1, source_target_pairs={{0,8},{8,0},{16,24},{24,16},{32,40},{40,32},{48,56},{56,48},{64,72... | collective-permute-start | bytes 3145736 | tf_op jit(solution)/shard_map/ppermute | solution.py:162
  10.6 0.0 copy-done.3
  10.6 0.6 dynamic_slice.18
  13.2 0.0 collective-permute-done
  13.2 1.1 select_select_fusion
  14.3 3.5 %all-to-all-start = ((bf16[32,2,64,128]{3,2,1,0:T(8,128)(2,1)}), bf16[32,2,64,128]{3,2,1,0:T(8,128)(2,1)S(1)}, u32[]{:S(2)}, u32[]{:S(2)}) async-start(bf16[32,2,64,128]{3,2,1,0:T(8,128)(2,1)} %select_select_fusion), calls=%async_computation | async-start | bytes 2097152 | tf_op jit(solution)/shard_map/all_to_all | solution.py:135
  17.8 13.7 %all-to-all-done = bf16[32,2,64,128]{3,2,1,0:T(8,128)(2,1)S(1)} async-done(((bf16[32,2,64,128]{3,2,1,0:T(8,128)(2,1)}), bf16[32,2,64,128]{3,2,1,0:T(8,128)(2,1)S(1)}, u32[]{:S(2)}, u32[]{:S(2)}) %all-to-all-start) | async-done | bytes 1048608 | tf_op jit(solution)/shard_map/all_to_all | solution.py:135
  31.6 0.0 copy-start
  31.6 0.0 copy-start.1
  31.6 0.0 copy-start.2
  31.6 40.9 %all-reduce.1 = bf16[8,2,64,128]{3,2,1,0:T(8,128)(2,1)S(1)} all-reduce(f32[8,2,64,128]{3,2,1,0:T(8,128)S(1)} %select_convert_fusion), channel_id=1, replica_groups={{0,64,128,192,256,320,384,448},{8,72,136,200,264,328,392,456},{16,80,14..., use_global_device_ids=true, to_apply=%region_0.1 | all-reduce | flops 131072 | bytes 786432 | tf_op jit(solution)/shard_map/psum | solution.py:166
  72.6 0.2 broadcast_in_dim.52
  72.8 11.9 %all_to_all.29.kv_ref.other_ref = bf16[32,2,64,128]{3,2,1,0:T(8,128)(2,1)S(1)} all-to-all(bf16[32,2,64,128]{3,2,1,0:T(8,128)(2,1)S(1)} %bitcast.11), channel_id=1, replica_groups={{0,16,32,48},{8,24,40,56},{64,80,96,112},{72,88,104,120},{128,144,160,1..., dimensions={0} | all-to-all | bytes 2097152 | tf_op jit(solution)/shard_map/all_to_all | solution.py:135
  84.7 10.7 %collective-permute-start.1 = (bf16[32,2,64,128]{3,2,1,0:T(8,128)(2,1)S(1)}, bf16[32,2,64,128]{3,2,1,0:T(8,128)(2,1)S(1)}, u32[]{:S(2)}, u32[]{:S(2)}) collective-permute-start(bf16[32,2,64,128]{3,2,1,0:T(8,128)(2,1)S(1)} %all_to_all.29.kv_ref.other_ref), channel_id=1, source_target_pairs={{0,8},{8,0},{16,24},{24,16},{32,40},{40,32},{48,56},{56,48},{64,72... | collective-permute-start | bytes 3145736 | tf_op jit(solution)/shard_map/ppermute | solution.py:168
  95.4 0.0 copy-done
  95.4 0.0 copy-done.1
  95.4 0.0 copy-done.2
  95.4 0.9 shard_map.64
  96.3 4.6 %shard_map.65.total_in = f32[8,256,256]{2,1,0:T(8,128)S(1)} custom-call(bf16[256,1024]{1,0:T(8,128)(2,1)S(1)} %copy-done, f32[8,256,128]{2,1,0:T(8,128)S(1)} %get-tuple-element.7.shift_ref, f32[8,256,256]{2,1,0:T(8,128)S(1)} %get-tuple-element.8.total_in, bf16[32,2,64,128]{3,2,1,0:T(8,128)(2,1)S(1)} %all_to_all.29.kv_ref.other_ref), custom_call_target="tpu_custom_call" | custom-call | flops 4294967296 | bytes 4194304 | tf_op jit(solution)/shard_map/pallas_call | solution.py:111
  101.0 0.0 collective-permute-done.1.kv_ref
  101.0 4.8 %shard_map.66 = bf16[256,1024]{1,0:T(8,128)(2,1)S(1)} custom-call(bf16[256,1024]{1,0:T(8,128)(2,1)S(1)} %copy-done, f32[8,256,128]{2,1,0:T(8,128)S(1)} %get-tuple-element.7.shift_ref, f32[8,256,256]{2,1,0:T(8,128)S(1)} %shard_map.65.total_in, bf16[32,2,64,128]{3,2,1,0:T(8,128)(2,1)S(1)} %collective-permute-done.1.kv_ref, bf16[256,128]{1,0:T(8,128)(2,1)S(1)} %copy-done.1, ...), custom_call_target="tpu_custom_call" | custom-call | flops 4294967296 | bytes 4194304 | tf_op jit(solution)/shard_map/pallas_call | solution.py:111
  105.8 17.0 %all_to_all.30 = bf16[8,32,1024]{2,1,0:T(8,128)(2,1)S(1)} all-to-all(bf16[8,32,1024]{2,1,0:T(8,128)(2,1)S(1)} %bitcast.10), channel_id=1, replica_groups=mesh['rep'=64,'tp'=8] {'tp'}, dimensions={0} | all-to-all | bytes 1048576 | tf_op jit(solution)/shard_map/all_to_all | solution.py:179
  122.8 0.8 copy.8
  (2 shorter events, 0.0 us)
Async XLA Ops:
  1.7 9.0 %copy-start.3 = (s32[8]{0:T(128)S(1)}, s32[8]{0:T(128)}, u32[]{:S(2)}) copy-start(s32[8]{0:T(128)} %param.6) | copy-start | bytes 100
  1.8 11.3 %collective-permute-start = (bf16[32,2,64,128]{3,2,1,0:T(8,128)(2,1)S(1)}, bf16[32,2,64,128]{3,2,1,0:T(8,128)(2,1)S(1)}, u32[]{:S(2)}, u32[]{:S(2)}) collective-permute-start(bf16[32,2,64,128]{3,2,1,0:T(8,128)(2,1)S(1)} %broadcast_select_fusion), channel_id=1, source_target_pairs={{0,8},{8,0},{16,24},{24,16},{32,40},{40,32},{48,56},{56,48},{64,72... | collective-permute-start | bytes 3145736 | tf_op jit(solution)/shard_map/ppermute | solution.py:162
  14.3 17.2 %all-to-all-start = ((bf16[32,2,64,128]{3,2,1,0:T(8,128)(2,1)}), bf16[32,2,64,128]{3,2,1,0:T(8,128)(2,1)S(1)}, u32[]{:S(2)}, u32[]{:S(2)}) async-start(bf16[32,2,64,128]{3,2,1,0:T(8,128)(2,1)} %select_select_fusion), calls=%async_computation | async-start | bytes 2097152 | tf_op jit(solution)/shard_map/all_to_all | solution.py:135
  31.6 63.8 %copy-start = (bf16[256,1024]{1,0:T(8,128)(2,1)S(1)}, bf16[256,1024]{1,0:T(8,128)(2,1)}, u32[]{:S(2)}) copy-start(bf16[256,1024]{1,0:T(8,128)(2,1)} %q_ref.5) | copy-start | bytes 1572868
  31.6 63.8 %copy-start.1 = (bf16[256,128]{1,0:T(8,128)(2,1)S(1)}, bf16[256,128]{1,0:T(8,128)(2,1)}, u32[]{:S(2)}) copy-start(bf16[256,128]{1,0:T(8,128)(2,1)} %k_ref.3) | copy-start | bytes 196612
  31.6 63.8 %copy-start.2 = (bf16[256,128]{1,0:T(8,128)(2,1)S(1)}, bf16[256,128]{1,0:T(8,128)(2,1)}, u32[]{:S(2)}) copy-start(bf16[256,128]{1,0:T(8,128)(2,1)} %v_ref.3) | copy-start | bytes 196612
  84.7 16.3 %collective-permute-start.1 = (bf16[32,2,64,128]{3,2,1,0:T(8,128)(2,1)S(1)}, bf16[32,2,64,128]{3,2,1,0:T(8,128)(2,1)S(1)}, u32[]{:S(2)}, u32[]{:S(2)}) collective-permute-start(bf16[32,2,64,128]{3,2,1,0:T(8,128)(2,1)S(1)} %all_to_all.29.kv_ref.other_ref), channel_id=1, source_target_pairs={{0,8},{8,0},{16,24},{24,16},{32,40},{40,32},{48,56},{56,48},{64,72... | collective-permute-start | bytes 3145736 | tf_op jit(solution)/shard_map/ppermute | solution.py:168

commit v4 on v3

--- a/solution.py
+++ b/solution.py
@@ -54,18 +54,15 @@
     return total
 
 
-def suffix_kernel(q_ref, k_ref, v_ref, shift_ref, total_ref):
+def first_kernel(q_ref, k_ref, v_ref, kv_ref, shift_ref, total_ref):
     for head in range(GROUP):
-        scores = suffix_scores(head_of(q_ref, head), k_ref[...])
+        query = head_of(q_ref, head)
+        scores = suffix_scores(query, k_ref[...])
         shift = jnp.broadcast_to(jnp.max(scores, axis=1, keepdims=True), (scores.shape[0], WIDTH))
         weights = jnp.exp2(scores - spread(shift, scores.shape[1] // WIDTH)).astype(bf16)
+        total = jnp.dot(weights, with_ones(v_ref[...]), preferred_element_type=f32)
         shift_ref[head] = shift
-        total_ref[head] = jnp.dot(weights, with_ones(v_ref[...]), preferred_element_type=f32)
-
-
-def next_kernel(q_ref, shift_ref, total_in, kv_ref, total_ref):
-    for head in range(GROUP):
-        total_ref[head] = add_piece(head_of(q_ref, head), shift_ref[head], kv_ref, total_in[head])
+        total_ref[head] = add_piece(query, shift, kv_ref, total)
 
 
 def last_kernel(q_ref, shift_ref, total_in, kv_ref, k_ref, v_ref, other_ref, out_ref):
@@ -134,10 +131,6 @@
     def exchange(array, groups):
         return lax.all_to_all(array, "rep", 0, 0, axis_index_groups=groups, tiled=True)
 
-    def pick(array, at, count):
-        share = array.shape[0] // count
-        return lax.dynamic_slice_in_dim(array, at * share, share, 0, allow_negative_indices=False)
-
     def copies(array, count):
         many = jnp.broadcast_to(array[None], (count, *array.shape))
         return many.reshape(count * array.shape[0], *array.shape[1:])
@@ -156,13 +149,15 @@
         )
         return jnp.where(is_key, keys, values)
 
-    in_near = (mine >> 1) & 3
     in_far = mine >> 3
-    owner_core = mine - 8 * in_far - 2 * in_near
+    share = half // 4
+    in_near = ((mine >> 1) & 3) * share
+    owner_core = mine - 8 * in_far - 2 * (in_near // share)
+    here = in_far == rep >> 3
     got = lax.ppermute(half_of(1 - core), "rep", swap_core)
-    part = jnp.where(owner_core == core, half_of(core), got)
-    part = pick(exchange(part, near), in_near, 4)
-    part = jnp.where(in_far == rep >> 3, part, jnp.zeros_like(part)).astype(f32)
+    part = jnp.where(here & (owner_core == core), half_of(owner_core), got)
+    part = lax.dynamic_slice_in_dim(exchange(part, near), in_near, share, 0, allow_negative_indices=False)
+    part = jnp.where(here, part, jnp.zeros_like(part)).astype(f32)
     part = lax.psum(part, "rep", axis_index_groups=far).astype(bf16)
     first = exchange(copies(part, 4), near)
     second = lax.ppermute(first, "rep", swap_core)
@@ -170,8 +165,7 @@
     shift_shape = jax.ShapeDtypeStruct((GROUP, rows, WIDTH), f32)
     total_shape = jax.ShapeDtypeStruct((GROUP, rows, 2 * WIDTH), f32)
     suffix = (rotated_suffix_keys, suffix_values)
-    shift, total = call(suffix_kernel, (shift_shape, total_shape), rows, queries, *suffix)
-    total = call(next_kernel, total_shape, half * PIECE, queries, shift, total, first)
+    shift, total = call(first_kernel, (shift_shape, total_shape), rows + half * PIECE, queries, *suffix, first)
     output = call(
         last_kernel, jax.ShapeDtypeStruct(queries.shape, bf16), half * PIECE,
         queries, shift, total, second, *suffix, first,

time: 124 us -> 126 us (1.016)
  blocking collectives: 69.9 us -> 85.2 us
  waiting for transfers between devices: 13.7 us -> 2.25 us
  starting transfers between devices: 23 us -> 21.6 us
    all_to_all x1 -> x2, blocking collectives: 11.9 us -> 28.2 us  [exchange(): lax.all_to_all(array, 'rep', 0, 0, axis_index_groups=groups, tiled=True)]
    all_to_all x1 -> x0, waiting for transfers between devices: 13.7 us -> none  [exchange(): lax.all_to_all(array, 'rep', 0, 0, axis_index_groups=groups, tiled=True)]
    all_to_all x1 -> x0, starting transfers between devices: 3.51 us -> none  [exchange(): lax.all_to_all(array, 'rep', 0, 0, axis_index_groups=groups, tiled=True)]
    ppermute x1, waiting for transfers between devices: 0.01 us -> 2.25 us  [local(): got = lax.ppermute(half_of(1 - core), 'rep', swap_core)]
    ppermute x1, starting transfers between devices: 10.7 us -> 12.8 us  [local(): second = lax.ppermute(first, 'rep', swap_core)]
    psum x1, blocking collectives: 40.9 us -> 39.4 us  [local(): part = lax.psum(part, 'rep', axis_index_groups=far).astype(bf16)]
    pallas_call x3 -> x2, Pallas kernels: 10.3 us -> 10 us  [call(): pl.pallas_call(kernel, in_specs=[in_vmem] * len(args), out_specs=jax.tree...]
  transfers between devices with their start and end apart: 3 -> 2, of which waited for: 1 -> 1; matrix products, arithmetic and copies ran while one was open for 0% -> 0% of each run, Pallas kernels for 4% -> 4%
where the time goes in v4:
time: 126 us
  blocking collectives  85.2 us (68%)
  starting transfers between devices  21.6 us (17%)
  Pallas kernels  10 us (8%)
  local copies, waits for them, and re-layouts  3.99 us (3%)
  waiting for transfers between devices  2.25 us (2%)
  between operations  2.12 us (2%)
    psum x1, blocking collectives, local(): part = lax.psum(part, 'rep', axis_index_groups=far).astype(bf16)  39.4 us
    all_to_all x2, blocking collectives, exchange(): lax.all_to_all(array, 'rep', 0, 0, axis_index_groups=groups, tiled=True)  28.2 us
    all_to_all x1, blocking collectives, local(): return lax.all_to_all(output, 'tp', split_axis=0, concat_axis=1, tiled=True)  17.6 us
    ppermute x1, starting transfers between devices, local(): second = lax.ppermute(first, 'rep', swap_core)  12.8 us
    pallas_call x2, Pallas kernels, call(): pl.pallas_call(kernel, in_specs=[in_vmem] * len(args), out_specs=jax.tree...  10 us
    ppermute x1, starting transfers between devices, local(): got = lax.ppermute(half_of(1 - core), 'rep', swap_core)  8.79 us
  transfers between devices with their start and end apart: 2, of which 1 were waited for; matrix products, arithmetic and copies ran while one was open for 0% of the time, Pallas kernels for 4%

profile of v4, /device:TPU:1, one launch (start us, length us, event | category | flops | bytes accessed | tf_op | source)
XLA Modules:
  0.0 125.5 jit_solution(5667139409201619324)
XLA Ops:
  0.0 1.2 dynamic_slice.18
  3.2 1.7 %constant_dynamic-slice_fusion.2 = (bf16[2048,128]{1,0:T(8,128)(2,1)S(1)}, bf16[2048,128]{1,0:T(8,128)(2,1)S(1)}, bf16[2048,128]{1,0:T(8,128)(2,1)S(1)}, bf16[2048,128]{1,0:T(8,128)(2,1)S(1)}) fusion(bf16[4096,128]{1,0:T(8,128)(2,1)} %param.11, s32[]{:T(128)S(6)} %mul.14, s32[]{:T(128)S(6)} %mul.15, bf16[4096,128]{1,0:T(8,128)(2,1)} %param.10), kind=kLoop, calls=%fused_computation.5 | loop fusion | bytes 4194312 | tf_op jit(solution)/shard_map/dynamic_slice | solution.py:147
  4.9 0.1 broadcast_select_fusion
  5.0 8.8 %collective-permute-start = (bf16[32,2,64,128]{3,2,1,0:T(8,128)(2,1)S(1)}, bf16[32,2,64,128]{3,2,1,0:T(8,128)(2,1)S(1)}, u32[]{:S(2)}, u32[]{:S(2)}) collective-permute-start(bf16[32,2,64,128]{3,2,1,0:T(8,128)(2,1)S(1)} %broadcast_select_fusion), channel_id=1, source_target_pairs={{0,8},{8,0},{16,24},{24,16},{32,40},{40,32},{48,56},{56,48},{64,72... | collective-permute-start | bytes 3145736 | tf_op jit(solution)/shard_map/ppermute | solution.py:157
  13.8 2.2 %collective-permute-done = bf16[32,2,64,128]{3,2,1,0:T(8,128)(2,1)S(1)} collective-permute-done((bf16[32,2,64,128]{3,2,1,0:T(8,128)(2,1)S(1)}, bf16[32,2,64,128]{3,2,1,0:T(8,128)(2,1)S(1)}, u32[]{:S(2)}, u32[]{:S(2)}) %collective-permute-start) | collective-permute-done | bytes 1048608 | tf_op jit(solution)/shard_map/ppermute | solution.py:157
  16.1 0.2 select_select_fusion
  16.3 16.0 %all_to_all.29 = bf16[32,2,64,128]{3,2,1,0:T(8,128)(2,1)S(1)} all-to-all(bf16[32,2,64,128]{3,2,1,0:T(8,128)(2,1)S(1)} %select_select_fusion), channel_id=1, replica_groups={{0,16,32,48},{8,24,40,56},{64,80,96,112},{72,88,104,120},{128,144,160,1..., dimensions={0} | all-to-all | bytes 2097152 | tf_op jit(solution)/shard_map/all_to_all | solution.py:132
  32.3 0.0 copy-start
  32.3 0.0 copy-start.1
  32.3 0.0 copy-start.2
  32.3 39.4 %all-reduce.1 = bf16[8,2,64,128]{3,2,1,0:T(8,128)(2,1)S(1)} all-reduce(f32[8,2,64,128]{3,2,1,0:T(8,128)S(1)} %select_convert_fusion), channel_id=1, replica_groups={{0,64,128,192,256,320,384,448},{8,72,136,200,264,328,392,456},{16,80,14..., use_global_device_ids=true, to_apply=%region_0.1 | all-reduce | flops 131072 | bytes 786432 | tf_op jit(solution)/shard_map/psum | solution.py:161
  71.7 0.2 broadcast_in_dim.52
  71.9 12.3 %all_to_all.30.kv_ref.other_ref = bf16[32,2,64,128]{3,2,1,0:T(8,128)(2,1)S(1)} all-to-all(bf16[32,2,64,128]{3,2,1,0:T(8,128)(2,1)S(1)} %bitcast.11), channel_id=1, replica_groups={{0,16,32,48},{8,24,40,56},{64,80,96,112},{72,88,104,120},{128,144,160,1..., dimensions={0} | all-to-all | bytes 2097152 | tf_op jit(solution)/shard_map/all_to_all | solution.py:132
  84.2 12.8 %collective-permute-start.1 = (bf16[32,2,64,128]{3,2,1,0:T(8,128)(2,1)S(1)}, bf16[32,2,64,128]{3,2,1,0:T(8,128)(2,1)S(1)}, u32[]{:S(2)}, u32[]{:S(2)}) collective-permute-start(bf16[32,2,64,128]{3,2,1,0:T(8,128)(2,1)S(1)} %all_to_all.30.kv_ref.other_ref), channel_id=1, source_target_pairs={{0,8},{8,0},{16,24},{24,16},{32,40},{40,32},{48,56},{56,48},{64,72... | collective-permute-start | bytes 3145736 | tf_op jit(solution)/shard_map/ppermute | solution.py:163
  97.0 0.0 copy-done
  97.0 0.0 copy-done.1
  97.0 0.0 copy-done.2
  97.0 5.3 %shard_map.64 = (f32[8,256,128]{2,1,0:T(8,128)S(1)}, f32[8,256,256]{2,1,0:T(8,128)S(1)}) custom-call(bf16[256,1024]{1,0:T(8,128)(2,1)S(1)} %copy-done, bf16[256,128]{1,0:T(8,128)(2,1)S(1)} %copy-done.1, bf16[256,128]{1,0:T(8,128)(2,1)S(1)} %copy-done.2, bf16[32,2,64,128]{3,2,1,0:T(8,128)(2,1)S(1)} %all_to_all.30.kv_ref.other_ref), custom_call_target="tpu_custom_call" | custom-call | flops 4831838208 | bytes 4194304 | tf_op jit(solution)/shard_map/pallas_call | solution.py:108
  102.3 0.0 collective-permute-done.1.kv_ref
  102.3 4.8 %shard_map.65 = bf16[256,1024]{1,0:T(8,128)(2,1)S(1)} custom-call(bf16[256,1024]{1,0:T(8,128)(2,1)S(1)} %copy-done, f32[8,256,128]{2,1,0:T(8,128)S(1)} %get-tuple-element.7.shift_ref, f32[8,256,256]{2,1,0:T(8,128)S(1)} %get-tuple-element.8.total_in, bf16[32,2,64,128]{3,2,1,0:T(8,128)(2,1)S(1)} %collective-permute-done.1.kv_ref, ...), custom_call_target="tpu_custom_call" | custom-call | flops 4294967296 | bytes 4194304 | tf_op jit(solution)/shard_map/pallas_call | solution.py:108
  107.1 17.6 %all_to_all.31 = bf16[8,32,1024]{2,1,0:T(8,128)(2,1)S(1)} all-to-all(bf16[8,32,1024]{2,1,0:T(8,128)(2,1)S(1)} %bitcast.10), channel_id=1, replica_groups=mesh['rep'=64,'tp'=8] {'tp'}, dimensions={0} | all-to-all | bytes 1048576 | tf_op jit(solution)/shard_map/all_to_all | solution.py:173
  124.7 0.8 copy.8
  (2 shorter events, 0.0 us)
Async XLA Ops:
  5.0 11.1 %collective-permute-start = (bf16[32,2,64,128]{3,2,1,0:T(8,128)(2,1)S(1)}, bf16[32,2,64,128]{3,2,1,0:T(8,128)(2,1)S(1)}, u32[]{:S(2)}, u32[]{:S(2)}) collective-permute-start(bf16[32,2,64,128]{3,2,1,0:T(8,128)(2,1)S(1)} %broadcast_select_fusion), channel_id=1, source_target_pairs={{0,8},{8,0},{16,24},{24,16},{32,40},{40,32},{48,56},{56,48},{64,72... | collective-permute-start | bytes 3145736 | tf_op jit(solution)/shard_map/ppermute | solution.py:157
  32.3 64.7 %copy-start = (bf16[256,1024]{1,0:T(8,128)(2,1)S(1)}, bf16[256,1024]{1,0:T(8,128)(2,1)}, u32[]{:S(2)}) copy-start(bf16[256,1024]{1,0:T(8,128)(2,1)} %q_ref.3) | copy-start | bytes 1572868
  32.3 64.7 %copy-start.1 = (bf16[256,128]{1,0:T(8,128)(2,1)S(1)}, bf16[256,128]{1,0:T(8,128)(2,1)}, u32[]{:S(2)}) copy-start(bf16[256,128]{1,0:T(8,128)(2,1)} %k_ref.3) | copy-start | bytes 196612
  32.3 64.7 %copy-start.2 = (bf16[256,128]{1,0:T(8,128)(2,1)S(1)}, bf16[256,128]{1,0:T(8,128)(2,1)}, u32[]{:S(2)}) copy-start(bf16[256,128]{1,0:T(8,128)(2,1)} %v_ref.3) | copy-start | bytes 196612
  84.2 18.1 %collective-permute-start.1 = (bf16[32,2,64,128]{3,2,1,0:T(8,128)(2,1)S(1)}, bf16[32,2,64,128]{3,2,1,0:T(8,128)(2,1)S(1)}, u32[]{:S(2)}, u32[]{:S(2)}) collective-permute-start(bf16[32,2,64,128]{3,2,1,0:T(8,128)(2,1)S(1)} %all_to_all.30.kv_ref.other_ref), channel_id=1, source_target_pairs={{0,8},{8,0},{16,24},{24,16},{32,40},{40,32},{48,56},{56,48},{64,72... | collective-permute-start | bytes 3145736 | tf_op jit(solution)/shard_map/ppermute | solution.py:163

commit v5 on v4

--- a/solution.py
+++ b/solution.py
@@ -155,7 +155,7 @@
     owner_core = mine - 8 * in_far - 2 * (in_near // share)
     here = in_far == rep >> 3
     got = lax.ppermute(half_of(1 - core), "rep", swap_core)
-    part = jnp.where(here & (owner_core == core), half_of(owner_core), got)
+    part = jnp.where(here & (owner_core == core), half_of(core), got)
     part = lax.dynamic_slice_in_dim(exchange(part, near), in_near, share, 0, allow_negative_indices=False)
     part = jnp.where(here, part, jnp.zeros_like(part)).astype(f32)
     part = lax.psum(part, "rep", axis_index_groups=far).astype(bf16)

time: 126 us -> 123 us (0.976)
  waiting for transfers between devices: 2.25 us -> 0.01 us
    ppermute x1, waiting for transfers between devices: 2.25 us -> 0.01 us  [local(): got = lax.ppermute(half_of(1 - core), 'rep', swap_core)]
  transfers between devices with their start and end apart: 2 -> 2, of which waited for: 1 -> 0; matrix products, arithmetic and copies ran while one was open for 0% -> 0% of each run, Pallas kernels for 4% -> 4%
where the time goes in v5:
time: 123 us; the launch traced here: 122 us
  blocking collectives  85.8 us (70%)
  starting transfers between devices  20.6 us (17%)
  Pallas kernels  10 us (8%)
  local copies, waits for them, and re-layouts  3.34 us (3%)
  between operations  2.11 us (2%)
    psum x1, blocking collectives, local(): part = lax.psum(part, 'rep', axis_index_groups=far).astype(bf16)  40.2 us
    all_to_all x2, blocking collectives, exchange(): lax.all_to_all(array, 'rep', 0, 0, axis_index_groups=groups, tiled=True)  28 us
    all_to_all x1, blocking collectives, local(): return lax.all_to_all(output, 'tp', split_axis=0, concat_axis=1, tiled=True)  17.6 us
    ppermute x1, starting transfers between devices, local(): second = lax.ppermute(first, 'rep', swap_core)  11.8 us
    pallas_call x2, Pallas kernels, call(): pl.pallas_call(kernel, in_specs=[in_vmem] * len(args), out_specs=jax.tree...  10 us
    ppermute x1, starting transfers between devices, local(): got = lax.ppermute(half_of(1 - core), 'rep', swap_core)  8.79 us
  transfers between devices with their start and end apart: 2, of which 0 were waited for; matrix products, arithmetic and copies ran while one was open for 0% of the time, Pallas kernels for 4%

profile of v5, /device:TPU:1, one launch (start us, length us, event | category | flops | bytes accessed | tf_op | source)
XLA Modules:
  0.0 122.3 jit_solution(6971396414999588574)
XLA Ops:
  0.0 1.7 %constant_dynamic-slice_fusion.2 = (bf16[2048,128]{1,0:T(8,128)(2,1)S(1)}, bf16[2048,128]{1,0:T(8,128)(2,1)S(1)}, bf16[2048,128]{1,0:T(8,128)(2,1)S(1)}, bf16[2048,128]{1,0:T(8,128)(2,1)S(1)}) fusion(bf16[4096,128]{1,0:T(8,128)(2,1)} %param.11, s32[]{:T(128)S(6)} %mul.14, s32[]{:T(128)S(6)} %mul.15, bf16[4096,128]{1,0:T(8,128)(2,1)} %param.10), kind=kLoop, calls=%fused_computation.5 | loop fusion | bytes 4194312 | tf_op jit(solution)/shard_map/dynamic_slice | solution.py:147
  1.7 0.0 copy-start.3
  1.7 0.1 broadcast_select_fusion
  1.8 8.8 %collective-permute-start = (bf16[32,2,64,128]{3,2,1,0:T(8,128)(2,1)S(1)}, bf16[32,2,64,128]{3,2,1,0:T(8,128)(2,1)S(1)}, u32[]{:S(2)}, u32[]{:S(2)}) collective-permute-start(bf16[32,2,64,128]{3,2,1,0:T(8,128)(2,1)S(1)} %broadcast_select_fusion), channel_id=1, source_target_pairs={{0,8},{8,0},{16,24},{24,16},{32,40},{40,32},{48,56},{56,48},{64,72... | collective-permute-start | bytes 3145736 | tf_op jit(solution)/shard_map/ppermute | solution.py:157
  10.6 0.0 copy-done.3
  10.6 0.6 dynamic_slice.18
  13.2 0.0 collective-permute-done
  13.2 0.2 select_select_fusion
  13.4 16.1 %all_to_all.29 = bf16[32,2,64,128]{3,2,1,0:T(8,128)(2,1)S(1)} all-to-all(bf16[32,2,64,128]{3,2,1,0:T(8,128)(2,1)S(1)} %select_select_fusion), channel_id=1, replica_groups={{0,16,32,48},{8,24,40,56},{64,80,96,112},{72,88,104,120},{128,144,160,1..., dimensions={0} | all-to-all | bytes 2097152 | tf_op jit(solution)/shard_map/all_to_all | solution.py:132
  29.5 0.0 copy-start
  29.5 0.0 copy-start.1
  29.5 0.0 copy-start.2
  29.6 40.2 %all-reduce.1 = bf16[8,2,64,128]{3,2,1,0:T(8,128)(2,1)S(1)} all-reduce(f32[8,2,64,128]{3,2,1,0:T(8,128)S(1)} %select_convert_fusion), channel_id=1, replica_groups={{0,64,128,192,256,320,384,448},{8,72,136,200,264,328,392,456},{16,80,14..., use_global_device_ids=true, to_apply=%region_0.1 | all-reduce | flops 131072 | bytes 786432 | tf_op jit(solution)/shard_map/psum | solution.py:161
  69.7 0.2 broadcast_in_dim.52
  70.0 11.9 %all_to_all.30.kv_ref.other_ref = bf16[32,2,64,128]{3,2,1,0:T(8,128)(2,1)S(1)} all-to-all(bf16[32,2,64,128]{3,2,1,0:T(8,128)(2,1)S(1)} %bitcast.11), channel_id=1, replica_groups={{0,16,32,48},{8,24,40,56},{64,80,96,112},{72,88,104,120},{128,144,160,1..., dimensions={0} | all-to-all | bytes 2097152 | tf_op jit(solution)/shard_map/all_to_all | solution.py:132
  81.9 11.8 %collective-permute-start.1 = (bf16[32,2,64,128]{3,2,1,0:T(8,128)(2,1)S(1)}, bf16[32,2,64,128]{3,2,1,0:T(8,128)(2,1)S(1)}, u32[]{:S(2)}, u32[]{:S(2)}) collective-permute-start(bf16[32,2,64,128]{3,2,1,0:T(8,128)(2,1)S(1)} %all_to_all.30.kv_ref.other_ref), channel_id=1, source_target_pairs={{0,8},{8,0},{16,24},{24,16},{32,40},{40,32},{48,56},{56,48},{64,72... | collective-permute-start | bytes 3145736 | tf_op jit(solution)/shard_map/ppermute | solution.py:163
  93.8 0.0 copy-done
  93.8 0.0 copy-done.1
  93.8 0.0 copy-done.2
  93.8 5.3 %shard_map.64 = (f32[8,256,128]{2,1,0:T(8,128)S(1)}, f32[8,256,256]{2,1,0:T(8,128)S(1)}) custom-call(bf16[256,1024]{1,0:T(8,128)(2,1)S(1)} %copy-done, bf16[256,128]{1,0:T(8,128)(2,1)S(1)} %copy-done.1, bf16[256,128]{1,0:T(8,128)(2,1)S(1)} %copy-done.2, bf16[32,2,64,128]{3,2,1,0:T(8,128)(2,1)S(1)} %all_to_all.30.kv_ref.other_ref), custom_call_target="tpu_custom_call" | custom-call | flops 4831838208 | bytes 4194304 | tf_op jit(solution)/shard_map/pallas_call | solution.py:108
  99.1 0.0 collective-permute-done.1.kv_ref
  99.1 4.8 %shard_map.65 = bf16[256,1024]{1,0:T(8,128)(2,1)S(1)} custom-call(bf16[256,1024]{1,0:T(8,128)(2,1)S(1)} %copy-done, f32[8,256,128]{2,1,0:T(8,128)S(1)} %get-tuple-element.7.shift_ref, f32[8,256,256]{2,1,0:T(8,128)S(1)} %get-tuple-element.8.total_in, bf16[32,2,64,128]{3,2,1,0:T(8,128)(2,1)S(1)} %collective-permute-done.1.kv_ref, ...), custom_call_target="tpu_custom_call" | custom-call | flops 4294967296 | bytes 4194304 | tf_op jit(solution)/shard_map/pallas_call | solution.py:108
  103.9 17.6 %all_to_all.31 = bf16[8,32,1024]{2,1,0:T(8,128)(2,1)S(1)} all-to-all(bf16[8,32,1024]{2,1,0:T(8,128)(2,1)S(1)} %bitcast.10), channel_id=1, replica_groups=mesh['rep'=64,'tp'=8] {'tp'}, dimensions={0} | all-to-all | bytes 1048576 | tf_op jit(solution)/shard_map/all_to_all | solution.py:173
  121.4 0.8 copy.8
  (2 shorter events, 0.0 us)
Async XLA Ops:
  1.7 9.0 %copy-start.3 = (s32[8]{0:T(128)S(1)}, s32[8]{0:T(128)}, u32[]{:S(2)}) copy-start(s32[8]{0:T(128)} %param.6) | copy-start | bytes 100
  1.8 11.4 %collective-permute-start = (bf16[32,2,64,128]{3,2,1,0:T(8,128)(2,1)S(1)}, bf16[32,2,64,128]{3,2,1,0:T(8,128)(2,1)S(1)}, u32[]{:S(2)}, u32[]{:S(2)}) collective-permute-start(bf16[32,2,64,128]{3,2,1,0:T(8,128)(2,1)S(1)} %broadcast_select_fusion), channel_id=1, source_target_pairs={{0,8},{8,0},{16,24},{24,16},{32,40},{40,32},{48,56},{56,48},{64,72... | collective-permute-start | bytes 3145736 | tf_op jit(solution)/shard_map/ppermute | solution.py:157
  29.5 64.2 %copy-start = (bf16[256,1024]{1,0:T(8,128)(2,1)S(1)}, bf16[256,1024]{1,0:T(8,128)(2,1)}, u32[]{:S(2)}) copy-start(bf16[256,1024]{1,0:T(8,128)(2,1)} %q_ref.3) | copy-start | bytes 1572868
  29.5 64.2 %copy-start.1 = (bf16[256,128]{1,0:T(8,128)(2,1)S(1)}, bf16[256,128]{1,0:T(8,128)(2,1)}, u32[]{:S(2)}) copy-start(bf16[256,128]{1,0:T(8,128)(2,1)} %k_ref.3) | copy-start | bytes 196612
  29.5 64.2 %copy-start.2 = (bf16[256,128]{1,0:T(8,128)(2,1)S(1)}, bf16[256,128]{1,0:T(8,128)(2,1)}, u32[]{:S(2)}) copy-start(bf16[256,128]{1,0:T(8,128)(2,1)} %v_ref.3) | copy-start | bytes 196612
  81.9 17.2 %collective-permute-start.1 = (bf16[32,2,64,128]{3,2,1,0:T(8,128)(2,1)S(1)}, bf16[32,2,64,128]{3,2,1,0:T(8,128)(2,1)S(1)}, u32[]{:S(2)}, u32[]{:S(2)}) collective-permute-start(bf16[32,2,64,128]{3,2,1,0:T(8,128)(2,1)S(1)} %all_to_all.30.kv_ref.other_ref), channel_id=1, source_target_pairs={{0,8},{8,0},{16,24},{24,16},{32,40},{40,32},{48,56},{56,48},{64,72... | collective-permute-start | bytes 3145736 | tf_op jit(solution)/shard_map/ppermute | solution.py:163

commit v6 on v5

--- a/solution.py
+++ b/solution.py
@@ -154,10 +154,19 @@
     in_near = ((mine >> 1) & 3) * share
     owner_core = mine - 8 * in_far - 2 * (in_near // share)
     here = in_far == rep >> 3
+
     got = lax.ppermute(half_of(1 - core), "rep", swap_core)
-    part = jnp.where(here & (owner_core == core), half_of(core), got)
-    part = lax.dynamic_slice_in_dim(exchange(part, near), in_near, share, 0, allow_negative_indices=False)
-    part = jnp.where(here, part, jnp.zeros_like(part)).astype(f32)
+    kept = half_of(core)
+
+    def scatter():
+        part = jnp.where(owner_core == core, kept, got)
+        part = exchange(part, near)
+        return lax.dynamic_slice_in_dim(part, in_near, share, 0, allow_negative_indices=False).astype(f32)
+
+    def nothing():
+        return jnp.zeros((share, 2, PIECE, WIDTH), f32)
+
+    part = lax.cond(here, scatter, nothing)
     part = lax.psum(part, "rep", axis_index_groups=far).astype(bf16)
     first = exchange(copies(part, 4), near)
     second = lax.ppermute(first, "rep", swap_core)

time: 123 us -> 121 us (0.984)
  starting transfers between devices: 20.6 us -> 18.4 us
  between operations: 2.11 us -> 0.83 us
    psum x1, blocking collectives: 40.2 us -> 59.9 us  [local(): part = lax.psum(part, 'rep', axis_index_groups=far).astype(bf16)]
    all_to_all x2 -> x1, blocking collectives: 28 us -> 11.9 us  [exchange(): lax.all_to_all(array, 'rep', 0, 0, axis_index_groups=groups, tiled=True)]
    all_to_all x1, blocking collectives: 17.6 us -> 14.6 us  [local(): return lax.all_to_all(output, 'tp', split_axis=0, concat_axis=1, tiled=True)]
    ppermute x1, starting transfers between devices: 11.8 us -> 9.64 us  [local(): second = lax.ppermute(first, 'rep', swap_core)]
  transfers between devices with their start and end apart: 2 -> 2, of which waited for: 0 -> 1; matrix products, arithmetic and copies ran while one was open for 0% -> 0% of each run, Pallas kernels for 4% -> 4%
where the time goes in v6:
time: 121 us; the launch traced here: 120 us
  blocking collectives  86.4 us (71%)
  starting transfers between devices  18.4 us (15%)
  Pallas kernels  10 us (8%)
  local copies, waits for them, and re-layouts  3.46 us (3%)
    psum x1, blocking collectives, local(): part = lax.psum(part, 'rep', axis_index_groups=far).astype(bf16)  59.9 us
    all_to_all x1, blocking collectives, local(): return lax.all_to_all(output, 'tp', split_axis=0, concat_axis=1, tiled=True)  14.6 us
    all_to_all x1, blocking collectives, exchange(): lax.all_to_all(array, 'rep', 0, 0, axis_index_groups=groups, tiled=True)  11.9 us
    pallas_call x2, Pallas kernels, call(): pl.pallas_call(kernel, in_specs=[in_vmem] * len(args), out_specs=jax.tree...  10 us
    ppermute x1, starting transfers between devices, local(): second = lax.ppermute(first, 'rep', swap_core)  9.64 us
    ppermute x1, starting transfers between devices, local(): got = lax.ppermute(half_of(1 - core), 'rep', swap_core)  8.77 us
  transfers between devices with their start and end apart: 2, of which 1 were waited for; matrix products, arithmetic and copies ran while one was open for 0% of the time, Pallas kernels for 4%

profile of v6, /device:TPU:1, one launch (start us, length us, event | category | flops | bytes accessed | tf_op | source)
XLA Modules:
  0.0 120.5 jit_solution(5238344768224968988)
XLA Ops:
  0.0 0.0 copy-start.5
  0.0 0.0 copy-start.3
  0.0 0.0 copy-start.4
  0.0 1.4 %constant_dynamic-slice_fusion.2 = (bf16[2048,128]{1,0:T(8,128)(2,1)S(1)}, bf16[2048,128]{1,0:T(8,128)(2,1)S(1)}) fusion(bf16[4096,128]{1,0:T(8,128)(2,1)} %param.13, s32[]{:T(128)S(6)} %mul.15, bf16[4096,128]{1,0:T(8,128)(2,1)} %param.12), kind=kLoop, calls=%fused_computation.6 | loop fusion | bytes 2097156 | tf_op jit(solution)/shard_map/dynamic_slice | solution.py:147
  1.5 0.1 broadcast_select_fusion
  1.6 8.8 %collective-permute-start = (bf16[32,2,64,128]{3,2,1,0:T(8,128)(2,1)S(1)}, bf16[32,2,64,128]{3,2,1,0:T(8,128)(2,1)}, u32[]{:S(2)}, u32[]{:S(2)}) collective-permute-start(bf16[32,2,64,128]{3,2,1,0:T(8,128)(2,1)S(1)} %broadcast_select_fusion), channel_id=1, source_target_pairs={{0,8},{8,0},{16,24},{24,16},{32,40},{40,32},{48,56},{56,48},{64,72... | collective-permute-start | bytes 3145736 | tf_op jit(solution)/shard_map/ppermute | solution.py:158
  10.4 0.0 copy-done.5
  10.4 0.6 dynamic_slice.22
  11.6 1.1 collective-permute-done
  12.8 0.3 iota.11
  13.1 0.0 copy-done.3
  13.1 0.0 copy-done.4
  13.1 0.1 conditional.1
  13.2 0.0 copy-start
  13.2 0.0 copy-start.1
  13.2 0.0 copy-start.2
  13.2 59.9 %all-reduce.1 = bf16[8,2,64,128]{3,2,1,0:T(8,128)(2,1)S(1)} all-reduce(f32[8,2,64,128]{3,2,1,0:T(8,128)S(1)} %get-tuple-element.98), channel_id=1, replica_groups={{0,64,128,192,256,320,384,448},{8,72,136,200,264,328,392,456},{16,80,14..., use_global_device_ids=true, to_apply=%region_2.3 | all-reduce | flops 131072 | bytes 786432 | tf_op jit(solution)/shard_map/psum | solution.py:170
  73.1 0.2 broadcast_in_dim.48
  73.4 11.9 %all_to_all.29.kv_ref.other_ref = bf16[32,2,64,128]{3,2,1,0:T(8,128)(2,1)S(1)} all-to-all(bf16[32,2,64,128]{3,2,1,0:T(8,128)(2,1)S(1)} %bitcast.11), channel_id=1, replica_groups={{0,16,32,48},{8,24,40,56},{64,80,96,112},{72,88,104,120},{128,144,160,1..., dimensions={0} | all-to-all | bytes 2097152 | tf_op jit(solution)/shard_map/all_to_all | solution.py:132
  85.3 9.6 %collective-permute-start.1 = (bf16[32,2,64,128]{3,2,1,0:T(8,128)(2,1)S(1)}, bf16[32,2,64,128]{3,2,1,0:T(8,128)(2,1)S(1)}, u32[]{:S(2)}, u32[]{:S(2)}) collective-permute-start(bf16[32,2,64,128]{3,2,1,0:T(8,128)(2,1)S(1)} %all_to_all.29.kv_ref.other_ref), channel_id=1, source_target_pairs={{0,8},{8,0},{16,24},{24,16},{32,40},{40,32},{48,56},{56,48},{64,72... | collective-permute-start | bytes 3145736 | tf_op jit(solution)/shard_map/ppermute | solution.py:172
  94.9 0.0 copy-done
  95.0 0.0 copy-done.1
  95.0 0.0 copy-done.2
  95.0 5.3 %shard_map.64 = (f32[8,256,128]{2,1,0:T(8,128)S(1)}, f32[8,256,256]{2,1,0:T(8,128)S(1)}) custom-call(bf16[256,1024]{1,0:T(8,128)(2,1)S(1)} %copy-done, bf16[256,128]{1,0:T(8,128)(2,1)S(1)} %copy-done.1, bf16[256,128]{1,0:T(8,128)(2,1)S(1)} %copy-done.2, bf16[32,2,64,128]{3,2,1,0:T(8,128)(2,1)S(1)} %all_to_all.29.kv_ref.other_ref), custom_call_target="tpu_custom_call" | custom-call | flops 4831838208 | bytes 4194304 | tf_op jit(solution)/shard_map/pallas_call | solution.py:108
  100.2 0.0 collective-permute-done.1.kv_ref
  100.3 4.8 %shard_map.65 = bf16[256,1024]{1,0:T(8,128)(2,1)S(1)} custom-call(bf16[256,1024]{1,0:T(8,128)(2,1)S(1)} %copy-done, f32[8,256,128]{2,1,0:T(8,128)S(1)} %get-tuple-element.84.shift_ref, f32[8,256,256]{2,1,0:T(8,128)S(1)} %get-tuple-element.85.total_in, bf16[32,2,64,128]{3,2,1,0:T(8,128)(2,1)S(1)} %collective-permute-done.1.kv_ref, ...), custom_call_target="tpu_custom_call" | custom-call | flops 4294967296 | bytes 4194304 | tf_op jit(solution)/shard_map/pallas_call | solution.py:108
  105.0 14.6 %all_to_all.30 = bf16[8,32,1024]{2,1,0:T(8,128)(2,1)S(1)} all-to-all(bf16[8,32,1024]{2,1,0:T(8,128)(2,1)S(1)} %bitcast.10), channel_id=1, replica_groups=mesh['rep'=64,'tp'=8] {'tp'}, dimensions={0} | all-to-all | bytes 1048576 | tf_op jit(solution)/shard_map/all_to_all | solution.py:182
  119.6 0.8 copy.8
  (2 shorter events, 0.0 us)
Async XLA Ops:
  0.0 10.4 %copy-start.5 = (s32[8]{0:T(128)S(1)}, s32[8]{0:T(128)}, u32[]{:S(2)}) copy-start(s32[8]{0:T(128)} %param.8) | copy-start | bytes 100
  0.0 13.1 %copy-start.3 = (bf16[4096,128]{1,0:T(8,128)(2,1)S(1)}, bf16[4096,128]{1,0:T(8,128)(2,1)}, u32[]{:S(2)}) copy-start(bf16[4096,128]{1,0:T(8,128)(2,1)} %param.12) | copy-start | bytes 3145732
  0.0 13.1 %copy-start.4 = (bf16[4096,128]{1,0:T(8,128)(2,1)S(1)}, bf16[4096,128]{1,0:T(8,128)(2,1)}, u32[]{:S(2)}) copy-start(bf16[4096,128]{1,0:T(8,128)(2,1)} %param.13) | copy-start | bytes 3145732
  1.6 11.2 %collective-permute-start = (bf16[32,2,64,128]{3,2,1,0:T(8,128)(2,1)S(1)}, bf16[32,2,64,128]{3,2,1,0:T(8,128)(2,1)}, u32[]{:S(2)}, u32[]{:S(2)}) collective-permute-start(bf16[32,2,64,128]{3,2,1,0:T(8,128)(2,1)S(1)} %broadcast_select_fusion), channel_id=1, source_target_pairs={{0,8},{8,0},{16,24},{24,16},{32,40},{40,32},{48,56},{56,48},{64,72... | collective-permute-start | bytes 3145736 | tf_op jit(solution)/shard_map/ppermute | solution.py:158
  13.2 81.8 %copy-start = (bf16[256,1024]{1,0:T(8,128)(2,1)S(1)}, bf16[256,1024]{1,0:T(8,128)(2,1)}, u32[]{:S(2)}) copy-start(bf16[256,1024]{1,0:T(8,128)(2,1)} %q_ref.3) | copy-start | bytes 1572868
  13.2 81.8 %copy-start.1 = (bf16[256,128]{1,0:T(8,128)(2,1)S(1)}, bf16[256,128]{1,0:T(8,128)(2,1)}, u32[]{:S(2)}) copy-start(bf16[256,128]{1,0:T(8,128)(2,1)} %k_ref.3) | copy-start | bytes 196612
  13.2 81.8 %copy-start.2 = (bf16[256,128]{1,0:T(8,128)(2,1)S(1)}, bf16[256,128]{1,0:T(8,128)(2,1)}, u32[]{:S(2)}) copy-start(bf16[256,128]{1,0:T(8,128)(2,1)} %v_ref.3) | copy-start | bytes 196612
  85.3 14.9 %collective-permute-start.1 = (bf16[32,2,64,128]{3,2,1,0:T(8,128)(2,1)S(1)}, bf16[32,2,64,128]{3,2,1,0:T(8,128)(2,1)S(1)}, u32[]{:S(2)}, u32[]{:S(2)}) collective-permute-start(bf16[32,2,64,128]{3,2,1,0:T(8,128)(2,1)S(1)} %all_to_all.29.kv_ref.other_ref), channel_id=1, source_target_pairs={{0,8},{8,0},{16,24},{24,16},{32,40},{40,32},{48,56},{56,48},{64,72... | collective-permute-start | bytes 3145736 | tf_op jit(solution)/shard_map/ppermute | solution.py:172

commit v7 on v5

--- a/solution.py
+++ b/solution.py
@@ -13,7 +13,7 @@
 GROUP = Q_HEADS // KEY_VALUE_HEADS
 WIDTH = 128
 PIECE = 64
-TILE = 1024
+TILE = 2048
 SCORE_SCALE = math.log2(math.e) / math.sqrt(WIDTH)
 NEGATIVE = -1e30
 LARGE = 1e30

time: 123 us -> 123 us (level)
  no operation moved by 1% of the time
where the time goes in v7:
time: 123 us; the launch traced here: 122 us
  blocking collectives  85.8 us (70%)
  starting transfers between devices  20.6 us (17%)
  Pallas kernels  10 us (8%)
  local copies, waits for them, and re-layouts  3.34 us (3%)
  between operations  2.11 us (2%)
    psum x1, blocking collectives, local(): part = lax.psum(part, 'rep', axis_index_groups=far).astype(bf16)  40.2 us
    all_to_all x2, blocking collectives, exchange(): lax.all_to_all(array, 'rep', 0, 0, axis_index_groups=groups, tiled=True)  28 us
    all_to_all x1, blocking collectives, local(): return lax.all_to_all(output, 'tp', split_axis=0, concat_axis=1, tiled=True)  17.6 us
    ppermute x1, starting transfers between devices, local(): second = lax.ppermute(first, 'rep', swap_core)  11.8 us
    pallas_call x2, Pallas kernels, call(): pl.pallas_call(kernel, in_specs=[in_vmem] * len(args), out_specs=jax.tree...  10 us
    ppermute x1, starting transfers between devices, local(): got = lax.ppermute(half_of(1 - core), 'rep', swap_core)  8.79 us
  transfers between devices with their start and end apart: 2, of which 0 were waited for; matrix products, arithmetic and copies ran while one was open for 0% of the time, Pallas kernels for 4%

profile of v7, /device:TPU:1, one launch (start us, length us, event | category | flops | bytes accessed | tf_op | source)
XLA Modules:
  0.0 122.3 jit_solution(17532236545573258552)
XLA Ops:
  0.0 1.7 %constant_dynamic-slice_fusion.2 = (bf16[2048,128]{1,0:T(8,128)(2,1)S(1)}, bf16[2048,128]{1,0:T(8,128)(2,1)S(1)}, bf16[2048,128]{1,0:T(8,128)(2,1)S(1)}, bf16[2048,128]{1,0:T(8,128)(2,1)S(1)}) fusion(bf16[4096,128]{1,0:T(8,128)(2,1)} %param.11, s32[]{:T(128)S(6)} %mul.14, s32[]{:T(128)S(6)} %mul.15, bf16[4096,128]{1,0:T(8,128)(2,1)} %param.10), kind=kLoop, calls=%fused_computation.5 | loop fusion | bytes 4194312 | tf_op jit(solution)/shard_map/dynamic_slice | solution.py:147
  1.7 0.0 copy-start.3
  1.7 0.1 broadcast_select_fusion
  1.8 8.8 %collective-permute-start = (bf16[32,2,64,128]{3,2,1,0:T(8,128)(2,1)S(1)}, bf16[32,2,64,128]{3,2,1,0:T(8,128)(2,1)S(1)}, u32[]{:S(2)}, u32[]{:S(2)}) collective-permute-start(bf16[32,2,64,128]{3,2,1,0:T(8,128)(2,1)S(1)} %broadcast_select_fusion), channel_id=1, source_target_pairs={{0,8},{8,0},{16,24},{24,16},{32,40},{40,32},{48,56},{56,48},{64,72... | collective-permute-start | bytes 3145736 | tf_op jit(solution)/shard_map/ppermute | solution.py:157
  10.6 0.0 copy-done.3
  10.6 0.6 dynamic_slice.18
  13.2 0.0 collective-permute-done
  13.2 0.2 select_select_fusion
  13.4 16.1 %all_to_all.29 = bf16[32,2,64,128]{3,2,1,0:T(8,128)(2,1)S(1)} all-to-all(bf16[32,2,64,128]{3,2,1,0:T(8,128)(2,1)S(1)} %select_select_fusion), channel_id=1, replica_groups={{0,16,32,48},{8,24,40,56},{64,80,96,112},{72,88,104,120},{128,144,160,1..., dimensions={0} | all-to-all | bytes 2097152 | tf_op jit(solution)/shard_map/all_to_all | solution.py:132
  29.5 0.0 copy-start
  29.5 0.0 copy-start.1
  29.5 0.0 copy-start.2
  29.6 40.2 %all-reduce.1 = bf16[8,2,64,128]{3,2,1,0:T(8,128)(2,1)S(1)} all-reduce(f32[8,2,64,128]{3,2,1,0:T(8,128)S(1)} %select_convert_fusion), channel_id=1, replica_groups={{0,64,128,192,256,320,384,448},{8,72,136,200,264,328,392,456},{16,80,14..., use_global_device_ids=true, to_apply=%region_0.1 | all-reduce | flops 131072 | bytes 786432 | tf_op jit(solution)/shard_map/psum | solution.py:161
  69.7 0.2 broadcast_in_dim.52
  70.0 11.9 %all_to_all.30.kv_ref.other_ref = bf16[32,2,64,128]{3,2,1,0:T(8,128)(2,1)S(1)} all-to-all(bf16[32,2,64,128]{3,2,1,0:T(8,128)(2,1)S(1)} %bitcast.11), channel_id=1, replica_groups={{0,16,32,48},{8,24,40,56},{64,80,96,112},{72,88,104,120},{128,144,160,1..., dimensions={0} | all-to-all | bytes 2097152 | tf_op jit(solution)/shard_map/all_to_all | solution.py:132
  81.9 11.8 %collective-permute-start.1 = (bf16[32,2,64,128]{3,2,1,0:T(8,128)(2,1)S(1)}, bf16[32,2,64,128]{3,2,1,0:T(8,128)(2,1)S(1)}, u32[]{:S(2)}, u32[]{:S(2)}) collective-permute-start(bf16[32,2,64,128]{3,2,1,0:T(8,128)(2,1)S(1)} %all_to_all.30.kv_ref.other_ref), channel_id=1, source_target_pairs={{0,8},{8,0},{16,24},{24,16},{32,40},{40,32},{48,56},{56,48},{64,72... | collective-permute-start | bytes 3145736 | tf_op jit(solution)/shard_map/ppermute | solution.py:163
  93.8 0.0 copy-done
  93.8 0.0 copy-done.1
  93.8 0.0 copy-done.2
  93.8 5.3 %shard_map.64 = (f32[8,256,128]{2,1,0:T(8,128)S(1)}, f32[8,256,256]{2,1,0:T(8,128)S(1)}) custom-call(bf16[256,1024]{1,0:T(8,128)(2,1)S(1)} %copy-done, bf16[256,128]{1,0:T(8,128)(2,1)S(1)} %copy-done.1, bf16[256,128]{1,0:T(8,128)(2,1)S(1)} %copy-done.2, bf16[32,2,64,128]{3,2,1,0:T(8,128)(2,1)S(1)} %all_to_all.30.kv_ref.other_ref), custom_call_target="tpu_custom_call" | custom-call | flops 4831838208 | bytes 4194304 | tf_op jit(solution)/shard_map/pallas_call | solution.py:108
  99.1 0.0 collective-permute-done.1.kv_ref
  99.1 4.8 %shard_map.65 = bf16[256,1024]{1,0:T(8,128)(2,1)S(1)} custom-call(bf16[256,1024]{1,0:T(8,128)(2,1)S(1)} %copy-done, f32[8,256,128]{2,1,0:T(8,128)S(1)} %get-tuple-element.7.shift_ref, f32[8,256,256]{2,1,0:T(8,128)S(1)} %get-tuple-element.8.total_in, bf16[32,2,64,128]{3,2,1,0:T(8,128)(2,1)S(1)} %collective-permute-done.1.kv_ref, ...), custom_call_target="tpu_custom_call" | custom-call | flops 4294967296 | bytes 4194304 | tf_op jit(solution)/shard_map/pallas_call | solution.py:108
  103.9 17.6 %all_to_all.31 = bf16[8,32,1024]{2,1,0:T(8,128)(2,1)S(1)} all-to-all(bf16[8,32,1024]{2,1,0:T(8,128)(2,1)S(1)} %bitcast.10), channel_id=1, replica_groups=mesh['rep'=64,'tp'=8] {'tp'}, dimensions={0} | all-to-all | bytes 1048576 | tf_op jit(solution)/shard_map/all_to_all | solution.py:173
  121.4 0.8 copy.8
  (2 shorter events, 0.0 us)
Async XLA Ops:
  1.7 9.0 %copy-start.3 = (s32[8]{0:T(128)S(1)}, s32[8]{0:T(128)}, u32[]{:S(2)}) copy-start(s32[8]{0:T(128)} %param.6) | copy-start | bytes 100
  1.8 11.4 %collective-permute-start = (bf16[32,2,64,128]{3,2,1,0:T(8,128)(2,1)S(1)}, bf16[32,2,64,128]{3,2,1,0:T(8,128)(2,1)S(1)}, u32[]{:S(2)}, u32[]{:S(2)}) collective-permute-start(bf16[32,2,64,128]{3,2,1,0:T(8,128)(2,1)S(1)} %broadcast_select_fusion), channel_id=1, source_target_pairs={{0,8},{8,0},{16,24},{24,16},{32,40},{40,32},{48,56},{56,48},{64,72... | collective-permute-start | bytes 3145736 | tf_op jit(solution)/shard_map/ppermute | solution.py:157
  29.5 64.2 %copy-start = (bf16[256,1024]{1,0:T(8,128)(2,1)S(1)}, bf16[256,1024]{1,0:T(8,128)(2,1)}, u32[]{:S(2)}) copy-start(bf16[256,1024]{1,0:T(8,128)(2,1)} %q_ref.3) | copy-start | bytes 1572868
  29.5 64.2 %copy-start.1 = (bf16[256,128]{1,0:T(8,128)(2,1)S(1)}, bf16[256,128]{1,0:T(8,128)(2,1)}, u32[]{:S(2)}) copy-start(bf16[256,128]{1,0:T(8,128)(2,1)} %k_ref.3) | copy-start | bytes 196612
  29.5 64.2 %copy-start.2 = (bf16[256,128]{1,0:T(8,128)(2,1)S(1)}, bf16[256,128]{1,0:T(8,128)(2,1)}, u32[]{:S(2)}) copy-start(bf16[256,128]{1,0:T(8,128)(2,1)} %v_ref.3) | copy-start | bytes 196612
  81.9 17.2 %collective-permute-start.1 = (bf16[32,2,64,128]{3,2,1,0:T(8,128)(2,1)S(1)}, bf16[32,2,64,128]{3,2,1,0:T(8,128)(2,1)S(1)}, u32[]{:S(2)}, u32[]{:S(2)}) collective-permute-start(bf16[32,2,64,128]{3,2,1,0:T(8,128)(2,1)S(1)} %all_to_all.30.kv_ref.other_ref), channel_id=1, source_target_pairs={{0,8},{8,0},{16,24},{24,16},{32,40},{40,32},{48,56},{56,48},{64,72... | collective-permute-start | bytes 3145736 | tf_op jit(solution)/shard_map/ppermute | solution.py:163
